TPU v7x, 32 devices: a whole 2x2x4 slice. The times are simulated.
32 devices in a mesh: ax: 4 (over y, x), circ: 8 (over z, core).
Axes of the slice: x: 2, y: 2, z: 4, core: 2. Of those that a mesh axis runs over, the one named last changes fastest.
Arguments:
- displace: float32 [3, 512, 16384], P(None, 'ax', 'circ'), may hold values from -6 to 6
- load: float32 [3, 512, 16384], P(None, 'ax', 'circ'), may hold values from -6 to 6
- history: float32 [9, 512, 16384], P(None, 'ax', 'circ'), may hold values from -4 to 4
- stiffen: float32 [512, 16384], P('ax', 'circ'), may hold values from 0.2 to 4
- modulus: float32 [9, 9], replicated, may hold values from -2 to 2
- radial_slope: float32 [32, 32], replicated, may hold values from -1 to 1
- radial_basis: float32 [32, 32], replicated, may hold values from -1 to 1
- axial_eig: float32 [512], replicated, may hold values from 0.05 to 4
- cycle_eig: float32 [512], replicated, may hold values from 0.05 to 4
- radial_eig: float32 [32], replicated, may hold values from 0.05 to 4
Outputs:
- precond: float32 [3, 512, 16384], P(None, ('ax', 'circ'))
All inputs are finite; a program needn't handle non-finite values.
Results may differ from a plain program's by a relative error of at most 0.000092.
Values sent between devices are 32-bit elements; how exact they have to be, the bound alone decides.
No kernel may reach another device: no remote copies, remote signals or barrier semaphores. Data moves between devices by JAX's collectives and lax.ppermute only.
A program may use at most 128 MiB of HBM per device.

v0:
```python
import math

import functools

import jax
import jax.numpy as jnp
import ml_dtypes
import numpy as np
from jax import lax
from jax.experimental import pallas as pl
from jax.experimental.pallas import tpu as pltpu
from jax.sharding import PartitionSpec as P

NA = 512
NC = 512
R = 32


def with_halo(block, sides, width, periodic):
    for axis, dim in sides:
        count = lax.axis_size(axis)
        forward = [(i, i + 1) for i in range(count - 1)]
        if periodic:
            forward.append((count - 1, 0))
        backward = [(target, source) for source, target in forward]
        low = lax.ppermute(
            lax.slice_in_dim(block, block.shape[dim] - width, None, axis=dim), axis, forward
        )
        high = lax.ppermute(lax.slice_in_dim(block, 0, width, axis=dim), axis, backward)
        block = jnp.concatenate([low, block, high], axis=dim)
    return block


def cycle_table(count):
    col = jnp.arange(count, dtype=jnp.int32)[:, None]
    mode = jnp.arange(count, dtype=jnp.int32)[None, :]
    half = count // 2
    folded = jnp.where(mode <= half, mode, mode - half)
    shift = jnp.where(mode <= half, 0.0, 0.5 * math.pi).astype(jnp.float32)
    scale_ends = jnp.where(
        (mode == 0) | (mode == half), math.sqrt(1.0 / count), math.sqrt(2.0 / count)
    ).astype(jnp.float32)
    phase = (col * folded % count).astype(jnp.float32) * (2.0 * math.pi / count)
    return jnp.cos(phase - shift) * scale_ends


def axial_table(rows, count):
    first = (rows + 1)[:, None]
    mode = jnp.arange(count, dtype=jnp.int32)[None, :] + 1
    phase = (first * mode % (2 * (count + 1))).astype(jnp.float32) * (math.pi / (count + 1))
    return jnp.sin(phase) * math.sqrt(2.0 / (count + 1))


def extend(field):
    rows = with_halo(field, (("ax", 1),), 1, False)
    return with_halo(rows, (("circ", 2),), R, True)


def cycle_parts(ext):
    span = ext.shape[2] - 2 * R
    left = ext[:, :, :span]
    middle = ext[:, :, R : R + span]
    right = ext[:, :, 2 * R :]
    return ((left + 4.0 * middle + right) / 6.0, (right - left) * 0.5)


def row_smooth(field):
    return (field[:, :-2] + 4.0 * field[:, 1:-1] + field[:, 2:]) / 6.0


def row_slope(field):
    return (field[:, 2:] - field[:, :-2]) * 0.5


def radial_mix(field, matrix, form):
    count, rows, flat = field.shape
    cube = field.reshape(count, rows, flat // R, R)
    mixed = jnp.einsum(form, cube, matrix, precision=lax.Precision.HIGHEST)
    return mixed.reshape(count, rows, flat)


def into_cycles(field):
    return lax.all_to_all(field, "circ", split_axis=1, concat_axis=2, tiled=True)


def cycle_forward(field, table, basis):
    count, rows, flat = field.shape
    cube = field.reshape(count * rows, NC, R)
    cube = jnp.einsum("bcr,ck->bkr", cube, table, precision=lax.Precision.HIGHEST)
    cube = jnp.einsum("bkr,rm->bkm", cube, basis, precision=lax.Precision.HIGHEST)
    return cube.reshape(count, rows, flat)


def cycle_inverse(field, table, basis):
    count, rows, flat = field.shape
    cube = field.reshape(count * rows, NC, R)
    cube = jnp.einsum("bkm,rm->bkr", cube, basis, precision=lax.Precision.HIGHEST)
    cube = jnp.einsum("bkr,ck->bcr", cube, table, precision=lax.Precision.HIGHEST)
    return cube.reshape(count, rows, flat)


def axial_solve(lines, forward_table, inverse_table, weights):
    modes = jnp.einsum("pk,cps->cks", forward_table, lines, precision=lax.Precision.HIGHEST)
    return jnp.einsum(
        "ak,cks->cas", inverse_table, modes * weights[None], precision=lax.Precision.HIGHEST
    )


def plain_body(
    displace,
    load,
    history,
    stiffen,
    modulus,
    radial_slope,
    radial_basis,
    axial_eig,
    cycle_eig,
    radial_eig,
):
    ext = extend(displace)
    cycle_v, cycle_d = cycle_parts(ext)
    smooth_v = row_smooth(cycle_v)
    radial_part = radial_mix(smooth_v, radial_slope, "iacq,rq->iacr")
    grads = jnp.concatenate([row_slope(cycle_v), row_smooth(cycle_d), radial_part], axis=0)
    mixed = jnp.einsum("mn,nac->mac", modulus, grads, precision=lax.Precision.HIGHEST)
    stress = (1.0 + stiffen)[None] * mixed + history
    ext_stress = extend(stress)
    first_v, unused_d = cycle_parts(ext_stress[0:3])
    unused_v, second_d = cycle_parts(ext_stress[3:6])
    third_v, unused_e = cycle_parts(ext_stress[6:9])
    third = radial_mix(row_smooth(third_v), radial_slope, "iacr,rq->iacq")
    pull = -row_slope(first_v) - row_smooth(second_d) + third
    resid = load - pull
    a_dev = displace.shape[1]
    flat_dev = displace.shape[2]
    n_ax = lax.axis_size("ax")
    n_circ = lax.axis_size("circ")
    piece = flat_dev // n_ax
    rows_cycle = a_dev // n_circ
    table_cycle = cycle_table(NC)
    spec = cycle_forward(into_cycles(resid), table_cycle, radial_basis)
    start = lax.axis_index("circ") * flat_dev + lax.axis_index("ax") * piece
    index_flat = start + jnp.arange(piece, dtype=jnp.int32)
    denom = (
        axial_eig[:, None]
        + jnp.take(cycle_eig, index_flat // R)[None, :]
        + jnp.take(radial_eig, index_flat % R)[None, :]
    )
    weights = 1.0 / denom
    natural_rows = jnp.arange(NA, dtype=jnp.int32)
    inverse_table = axial_table(natural_rows, NA)
    cube = spec.reshape(3, rows_cycle, n_circ, flat_dev)
    lines = lax.all_to_all(
        lax.all_to_all(cube, "ax", split_axis=3, concat_axis=1, tiled=True),
        "circ",
        split_axis=2,
        concat_axis=1,
        tiled=True,
    ).reshape(3, NA, piece)
    group = n_ax * rows_cycle
    outer = natural_rows // group
    inner = natural_rows % group
    source_rows = inner // rows_cycle * a_dev + outer * rows_cycle + inner % rows_cycle
    forward_table = axial_table(source_rows, NA)
    solved = axial_solve(lines, forward_table, inverse_table, weights)
    cycles_back = lax.all_to_all(
        lax.all_to_all(solved, "ax", split_axis=1, concat_axis=2, tiled=True),
        "circ",
        split_axis=1,
        concat_axis=2,
        tiled=True,
    )
    return cycle_inverse(cycles_back, table_cycle, radial_basis)


BF = jnp.bfloat16
F32 = jnp.float32
VMEM = pl.BlockSpec(memory_space=pltpu.VMEM)
SMEM = pl.BlockSpec(memory_space=pltpu.SMEM)
HBM = pl.BlockSpec(memory_space=pltpu.HBM)
HALO = 8
PAD = 8
HALF = 64
LANES = 128


def params(mebibytes=60):
    return pltpu.CompilerParams(vmem_limit_bytes=mebibytes << 20)


def cost(microseconds):
    return pl.CostEstimate(flops=1, bytes_accessed=int(microseconds * 3.6e6) + 1, transcendentals=0)


def split(x):
    hi = x.astype(BF)
    return hi, (x - hi.astype(F32)).astype(BF)


def dot(a, b, transposed=False):
    dims = (((1,), (1 if transposed else 0,)), ((), ()))
    return lax.dot_general(a, b, dims, preferred_element_type=F32)


def dot3(ah, al, bh, bl, transposed=False):
    return dot(ah, bh, transposed) + (dot(ah, bl, transposed) + dot(al, bh, transposed))


def stacked3(both, bh, bl, transposed=False):
    rows = both.shape[0] // 2
    upper = dot(both[...], bh, transposed)
    return upper[:rows] + (upper[rows:] + dot(both[0:rows, :], bl, transposed))


def exact(a, b, transposed=False):
    dims = (((1,), (1 if transposed else 0,)), ((), ()))
    return lax.dot_general(
        a, b, dims, precision=lax.Precision.HIGHEST, preferred_element_type=F32
    )


def host_split(table):
    hi = table.astype(np.float32).astype(ml_dtypes.bfloat16)
    lo = (table - hi.astype(np.float64)).astype(np.float32).astype(ml_dtypes.bfloat16)
    return jnp.asarray(np.concatenate([hi, lo], axis=0))


def host_cycle(count):
    col = np.arange(count)[None, :]
    mode = np.arange(count)[:, None]
    half = count // 2
    folded = np.where(mode <= half, mode, mode - half)
    phase = 2.0 * np.pi * ((col * folded) % count) / count
    scale = np.where((mode == 0) | (mode == half), math.sqrt(1.0 / count), math.sqrt(2.0 / count))
    return np.where(mode <= half, np.cos(phase), np.sin(phase)) * scale


def host_axial(count):
    first = np.arange(1, count + 1)
    phase = np.pi * (np.outer(first, first) % (2 * (count + 1))) / (count + 1)
    return np.sin(phase) * math.sqrt(2.0 / (count + 1))


def host_weave(mp):
    table = np.zeros((mp * LANES, mp * LANES), np.float32)
    for m in range(mp):
        for c in range(LANES):
            table[m * LANES + c, c * mp + m] = 1.0
    return jnp.asarray(table.astype(ml_dtypes.bfloat16))


def iota(shape, dim):
    return lax.broadcasted_iota(jnp.int32, shape, dim)


def onehot(condition):
    return jnp.where(condition, 1.0, 0.0).astype(F32)


def write_split(hi_ref, lo_ref, value):
    hi, lo = split(value)
    hi_ref[...] = hi
    lo_ref[...] = lo


def fetch(sources, targets, sems):
    copies = [
        pltpu.make_async_copy(source, target, sems.at[k])
        for k, (source, target) in enumerate(zip(sources, targets, strict=True))
    ]
    for copy in copies:
        copy.start()
    return copies


def write_stack(ref, value):
    rows = value.shape[0]
    hi, lo = split(value)
    ref[0:rows, :] = hi
    ref[rows:, :] = lo


def fetch(sources, targets, sems):
    copies = [
        pltpu.make_async_copy(source, target, sems.at[k])
        for k, (source, target) in enumerate(zip(sources, targets, strict=True))
    ]
    for copy in copies:
        copy.start()
    return copies


def front_tables_kernel(mp, slope_ref, basis_ref, *refs):
    outs, made, sems = refs[:6], refs[6:12], refs[12]
    krh, krl, kbh, kbl, kwh, kwl = made
    slope = slope_ref[...]
    basis = basis_ref[...]
    side = LANES
    row = iota((side, R), 0)
    col = iota((side, R), 1)
    pick = onehot(row % R == col)
    mask = iota((side, side), 0) // R == iota((side, side), 1) // R
    value = exact(exact(pick, slope, True), pick, True)
    write_split(krh, krl, jnp.where(mask, value * (1.0 / 36.0), 0.0))
    side = 8 * R
    row = iota((side, R), 0)
    col = iota((side, R), 1)
    pick = onehot(row % R == col)
    block = mp * 8
    mode = onehot(row // block * mp + (row % block) // 8 == col)
    mask = iota((side, side), 0) % 8 == iota((side, side), 1) // R
    value = exact(exact(mode, basis, True), pick, True)
    write_split(kbh, kbl, jnp.where(mask, value, 0.0))
    both = exact(slope, basis)
    value = exact(exact(mode, both, True), pick, True)
    write_split(kwh, kwl, jnp.where(mask, value * (-1.0 / 36.0), 0.0))
    for copy in fetch(made, outs, sems):
        copy.wait()


def front_tables(slope, basis, mp):
    one = jax.ShapeDtypeStruct((LANES, LANES), BF)
    two = jax.ShapeDtypeStruct((8 * R, 8 * R), BF)
    return pl.pallas_call(
        functools.partial(front_tables_kernel, mp),
        out_shape=(one, one, two, two, two, two),
        in_specs=[VMEM, VMEM],
        out_specs=(HBM,) * 6,
        scratch_shapes=[pltpu.VMEM(x.shape, BF) for x in (one, one, two, two, two, two)]
        + [pltpu.SemaphoreType.DMA((6,))],
        compiler_params=params(),
        name="front_tables",
    )(slope, basis)


def back_tables_kernel(mp, basis_ref, after, out, made, sem):
    del after
    rows, cols = made.shape[0] // 2, made.shape[1]
    row = iota((rows, R), 0)
    col = iota((rows, R), 1)
    mode = onehot(row // HALF * mp + row % mp == col)
    pick = onehot(iota((cols, R), 0) % R == iota((cols, R), 1))
    value = exact(exact(mode, basis_ref[...], True), pick, True)
    mask = (iota((rows, cols), 0) % HALF) // mp == iota((rows, cols), 1) // R
    write_stack(made, jnp.where(mask, value, 0.0))
    copy = pltpu.make_async_copy(made, out, sem)
    copy.start()
    copy.wait()


def back_tables(basis, mp, peers, after):
    shape = jax.ShapeDtypeStruct((2 * peers * HALF, HALF // mp * R), BF)
    return pl.pallas_call(
        functools.partial(back_tables_kernel, mp),
        out_shape=shape,
        in_specs=[VMEM, HBM],
        out_specs=HBM,
        scratch_shapes=[pltpu.VMEM(shape.shape, BF), pltpu.SemaphoreType.DMA],
        compiler_params=params(24),
        name="back_tables",
    )(basis, after)


def pack_columns(out, lane, wide, slim, pieces):
    for tile in range(4):
        value = None
        for index, piece in enumerate(pieces):
            at = 64 * index if index < 3 else 96 + 32 * index
            if at // LANES == tile:
                shift = (at - (wide if index < 3 else slim)) % LANES
                moved = pltpu.roll(piece, shift, 1) if shift else piece
                value = moved if value is None else jnp.where(lane >= at % LANES, moved, value)
        out[:, tile * LANES : (tile + 1) * LANES] = value


def pack_kernel(
    displace, history, stiffen, up_ref, down_ref, left_ref, right_ref, d, h, s, dc, hc, sc, sems
):
    rows, flat = stiffen.shape
    sources, targets = [], []
    for k, at in enumerate((slice(0, 8), slice(rows - 8, rows))):
        sources += [displace.at[:, at, :], history.at[:, at, :], stiffen.at[at, :]]
        targets += [d.at[k], h.at[k], s.at[k]]
    for k, at in enumerate((slice(0, LANES), slice(flat - LANES, flat))):
        sources += [displace.at[:, :, at], history.at[:, :, at], stiffen.at[:, at]]
        targets += [dc.at[k], hc.at[k], sc.at[k]]
    copies = fetch(sources, targets, sems)
    for copy in copies[:6]:
        copy.wait()
    for k, first, last, out in ((0, 0, 0, up_ref), (1, 6, 7, down_ref)):
        for i in range(3):
            out[2 * i : 2 * i + 2, :] = d[k, i, first : first + 2, :]
        for n in range(9):
            out[6 + n : 7 + n, :] = h[k, n, last : last + 1, :]
        out[15:16, :] = 1.0 + s[k, last : last + 1, :]
    for copy in copies[6:]:
        copy.wait()
    lane = iota((rows, LANES), 1)
    for k, out, wide, slim in ((0, left_ref, 0, 0), (1, right_ref, LANES - 2 * R, LANES - R)):
        pieces = [dc[k, i] for i in range(3)] + [hc[k, n] for n in range(9)] + [1.0 + sc[k]]
        pack_columns(out, lane, wide, slim, pieces)


def pack(displace, history, stiffen):
    rows, flat = stiffen.shape
    row = jax.ShapeDtypeStruct((16, flat), F32)
    column = jax.ShapeDtypeStruct((rows, 4 * LANES), F32)
    return pl.pallas_call(
        pack_kernel,
        out_shape=(row, row, column, column),
        in_specs=[HBM] * 3,
        out_specs=(VMEM,) * 4,
        scratch_shapes=[
            pltpu.VMEM((2, 3, 8, flat), F32),
            pltpu.VMEM((2, 9, 8, flat), F32),
            pltpu.VMEM((2, 8, flat), F32),
            pltpu.VMEM((2, 3, rows, LANES), F32),
            pltpu.VMEM((2, 9, rows, LANES), F32),
            pltpu.VMEM((2, rows, LANES), F32),
            pltpu.SemaphoreType.DMA((12,)),
        ],
        compiler_params=params(60),
        cost_estimate=cost(0),
        name="pack",
    )(displace, history, stiffen)


def corners_kernel(top, bottom, after, left_ref, right_ref, tall):
    del after
    flat = top.shape[1]
    lane = iota((HALO, LANES), 1)
    tall[...] = jnp.zeros_like(tall)
    for out, at, wide, slim in (
        (left_ref, slice(0, LANES), 0, 0),
        (right_ref, slice(flat - LANES, flat), LANES - 2 * R, LANES - R),
    ):
        pieces = []
        for index in range(13):
            first, count = (2 * index, 2) if index < 3 else (3 + index, 1)
            tall[index, 0:count, :] = bottom[first : first + count, at]
            tall[index, HALO - count : HALO, :] = top[first : first + count, at]
            pieces.append(tall[index])
        pack_columns(out, lane, wide, slim, pieces)


def corners(top, bottom, after):
    shape = jax.ShapeDtypeStruct((HALO, 4 * LANES), F32)
    return pl.pallas_call(
        corners_kernel,
        out_shape=(shape, shape),
        in_specs=[VMEM] * 2 + [HBM],
        out_specs=(VMEM, VMEM),
        scratch_shapes=[pltpu.VMEM((13, HALO, LANES), F32)],
        compiler_params=params(),
        cost_estimate=cost(0),
        name="corners",
    )(top, bottom, after)


def stencil_kernel(
    comps,
    mp,
    peers,
    modulus,
    displace,
    load,
    history,
    stiffen,
    top,
    bottom,
    left,
    left_corner,
    right,
    right_corner,
    *rest,
):
    n = len(comps)
    out, xd, hx, sx, ld, st, sums, diffs, made, krh, krl, kbh, kbl, kwh, kwl, sems = rest[7:]
    rows, flat = stiffen.shape
    tall = rows + HALO
    tiles = flat // LANES
    entries = [comp + 3 * k for comp in comps for k in range(3)]
    center = (slice(0, rows), slice(0, flat))

    def displace_copy(i, t):
        return pltpu.make_async_copy(
            displace.at[i, :, t * LANES : (t + 1) * LANES],
            xd.at[i, t, PAD : PAD + rows, :],
            sems.at[i * tiles + t],
        )

    moves = [displace_copy(i, t) for t in range(tiles) for i in range(3)]
    base = 3 * tiles
    late = [pltpu.make_async_copy(stiffen, sx.at[center], sems.at[base])]
    late += [
        pltpu.make_async_copy(history.at[m], hx.at[(k,) + center], sems.at[base + 1 + k])
        for k, m in enumerate(entries)
    ]
    final = [
        pltpu.make_async_copy(load.at[comp], ld.at[k], sems.at[base + 1 + 3 * n + k])
        for k, comp in enumerate(comps)
    ]
    tables = [
        pltpu.make_async_copy(source, target, sems.at[base + 1 + 5 * n + k])
        for k, (source, target) in enumerate(
            zip(rest[:6], (krh, krl, kbh, kbl, kwh, kwl), strict=True)
        )
    ]
    late += tables[:2]
    final += tables[2:]
    for copy in moves + late + final:
        copy.start()
    left = (left, left_corner)
    right = (right, right_corner)
    lane = iota((tall, LANES), 1)
    short = iota((rows, LANES), 1)

    def tile_of(refs, at, target):
        part = slice(at // LANES * LANES, (at // LANES + 1) * LANES)
        value = jnp.concatenate([ref[:, part] for ref in refs], axis=0)
        shift = (target - at) % LANES
        return pltpu.roll(value, shift, 1) if shift else value

    for i in range(3):
        tile = jnp.where(lane < 64, tile_of(right, 64 * i, 0), tile_of(left, 64 * i, 64))
        xd[i, tiles, PAD : PAD + tall, :] = tile
        xd[i, tiles, PAD - 1 : PAD, :] = tile[tall - 1 : tall]
        xd[i, tiles, PAD + tall : PAD + tall + 1, :] = tile[0:1]
        for t in range(tiles):
            part = slice(t * LANES, (t + 1) * LANES)
            above = top[2 * i : 2 * i + 2, part]
            xd[i, t, PAD + rows : PAD + rows + 2, :] = bottom[2 * i : 2 * i + 2, part]
            xd[i, t, PAD + tall - 2 : PAD + tall, :] = above
            xd[i, t, PAD - 1 : PAD, :] = above[1:2]
    zeros = jnp.zeros((HALO, flat), F32)
    for k, m in enumerate(entries):
        at = 192 + 32 * m
        hx[k, rows:tall, 0:flat] = zeros
        hx[k, rows : rows + 1, 0:flat] = bottom[6 + m : 7 + m, :]
        hx[k, tall - 1 : tall, 0:flat] = top[6 + m : 7 + m, :]
        hx[k, :, flat:] = jnp.where(lane < 64, tile_of(right, at, 0), tile_of(left, at, 96))
    sx[rows:tall, 0:flat] = zeros
    sx[rows : rows + 1, 0:flat] = bottom[15:16, :] - 1.0
    sx[tall - 1 : tall, 0:flat] = top[15:16, :] - 1.0
    sx[:, flat:] = jnp.where(lane < 64, tile_of(right, 480, 0), tile_of(left, 480, 96)) - 1.0

    def lanes(t):
        return pl.ds(pl.multiple_of(t * LANES, LANES), LANES)

    def previous(t):
        return lax.rem(t + tiles, tiles + 1)

    def following(t):
        return lax.rem(t + 1, tiles + 1)

    def lower(ref, k, t, height, mask):
        mixed = jnp.where(
            mask >= LANES - R, ref[k, previous(t), 0:height, :], ref[k, t, 0:height, :]
        )
        return pltpu.roll(mixed, R, 1)

    def higher(ref, k, t, height, mask):
        mixed = jnp.where(mask < R, ref[k, following(t), 0:height, :], ref[k, t, 0:height, :])
        return pltpu.roll(mixed, LANES - R, 1)

    for copy in moves:
        copy.wait()

    def rows_step(t, carry):
        for i in range(3):
            xd[i, t, PAD + tall : PAD + tall + 1, :] = xd[i, t, PAD : PAD + 1, :]
            above = xd[i, t, PAD - 1 : PAD - 1 + tall, :]
            below = xd[i, t, PAD + 1 : PAD + 1 + tall, :]
            total = above + 4.0 * xd[i, t, PAD : PAD + tall, :] + below
            change = below - above
            sums[i, t] = total
            diffs[i, t] = change
        return carry

    lax.fori_loop(0, tiles + 1, rows_step, 0)
    for copy in late:
        copy.wait()

    def stress_step(t, carry):
        total = [None] * len(entries)
        for i in range(3):
            low = lower(sums, i, t, tall, lane)
            high = higher(sums, i, t, tall, lane)
            second = high - low
            both = low + high + 4.0 * sums[i, t]
            low = lower(diffs, i, t, tall, lane)
            high = higher(diffs, i, t, tall, lane)
            first = low + high + 4.0 * diffs[i, t]
            bh, bl = split(both)
            third = dot3(bh, bl, krh[...], krl[...])
            for k, m in enumerate(entries):
                part = (
                    (modulus[m, i] * (1.0 / 12.0)) * first
                    + (modulus[m, 3 + i] * (1.0 / 12.0)) * second
                    + modulus[m, 6 + i] * third
                )
                total[k] = part if total[k] is None else total[k] + part
        factor = 1.0 + sx[:, lanes(t)]
        for k in range(len(entries)):
            value = factor * total[k] + hx[k, :, lanes(t)]
            st[k, t, PAD : PAD + tall, :] = value
            st[k, t, PAD - 1 : PAD, :] = value[tall - 1 : tall]
        return carry

    def stress_steps(s, carry):
        stress_step(2 * s + 0, carry)
        stress_step(2 * s + 1, carry)
        return carry

    if n == 1:
        lax.fori_loop(0, tiles + 1, stress_step, 0, unroll=True)
    else:
        lax.fori_loop(0, tiles // 2, stress_steps, 0)
        stress_step(tiles, 0)
    for copy in final:
        copy.wait()

    sent = []
    for index in range(n):
        first_entry = 3 * index
        message = made.at[index]

        def pull_rows(t, carry):
            def around(k):
                field = first_entry + k
                return (
                    st[field, t, PAD - 1 : PAD - 1 + rows, :],
                    st[field, t, PAD : PAD + rows, :],
                    st[field, t, PAD + 1 : PAD + 1 + rows, :],
                )

            above, _, below = around(0)
            p = below - above
            above, now, below = around(1)
            q = above + 4.0 * now + below
            above, now, below = around(2)
            w = above + 4.0 * now + below
            sums[0, t, 0:rows, :] = p - q
            sums[1, t, 0:rows, :] = p + q
            sums[2, t, 0:rows, :] = w
            return carry

        lax.fori_loop(0, tiles + 1, pull_rows, 0)

        def message_step(s, carry):
            us, ws = [], []
            for half in range(2):
                t = 2 * s + half
                pull = 2.0 * (sums[0, t, 0:rows, :] + sums[1, t, 0:rows, :])
                pull = pull + lower(sums, 0, t, rows, short) + higher(sums, 1, t, rows, short)
                us.append(ld[index, :, lanes(t)] + pull * (1.0 / 12.0))
                w = 4.0 * sums[2, t, 0:rows, :]
                ws.append(w + lower(sums, 2, t, rows, short) + higher(sums, 2, t, rows, short))
            uh, ul = split(jnp.concatenate(us, axis=1))
            wh, wl = split(jnp.concatenate(ws, axis=1))
            value = dot3(kbh[...], kbl[...], uh, ul, True)
            value = value + dot3(kwh[...], kwl[...], wh, wl, True)
            here = pl.ds(pl.multiple_of(s * 8, 8), 8)
            for peer in range(peers):
                for m in range(mp):
                    row = (peer * mp + m) * 8
                    message[peer, here, m * rows : (m + 1) * rows] = value[row : row + 8, :]
            return carry

        def message_pair(s, carry):
            message_step(2 * s, carry)
            return message_step(2 * s + 1, carry)

        if n == 1:
            lax.fori_loop(0, tiles // 2, message_step, 0, unroll=True)
        else:
            lax.fori_loop(0, tiles // 4, message_pair, 0)
        sent += [pltpu.make_async_copy(message, out.at[:, index], sems.at[base + 1 + 4 * n + index])]
        sent[-1].start()
    for copy in sent:
        copy.wait()


def stencil(comps, mp, peers, modulus, displace, load, history, stiffen, halos, tables, after):
    rows, flat = stiffen.shape
    tall = rows + HALO
    wide = flat + LANES
    tiles = flat // LANES
    n = len(comps)
    block = (flat // R, mp * rows)
    return pl.pallas_call(
        functools.partial(stencil_kernel, comps, mp, peers),
        out_shape=jax.ShapeDtypeStruct((peers, n) + block, F32),
        in_specs=[SMEM] + [HBM] * 4 + [VMEM] * 6 + [HBM] * 7,
        out_specs=HBM,
        scratch_shapes=[
            pltpu.VMEM((3, tiles + 1, PAD + tall + HALO, LANES), F32),
            pltpu.VMEM((3 * n, tall, wide), F32),
            pltpu.VMEM((tall, wide), F32),
            pltpu.VMEM((n, rows, flat), F32),
            pltpu.VMEM((3 * n, tiles + 1, PAD + tall, LANES), F32),
            pltpu.VMEM((3, tiles + 1, tall, LANES), F32),
            pltpu.VMEM((3, tiles + 1, tall, LANES), F32),
            pltpu.VMEM((n, peers) + block, F32),
            *(pltpu.VMEM(table.shape, BF) for table in tables),
            pltpu.SemaphoreType.DMA((3 * tiles + 7 + 5 * n,)),
        ],
        compiler_params=params(),
        cost_estimate=cost(13 + 8 * n),
        name="stencil",
    )(modulus, displace, load, history, stiffen, *halos, *tables, after)


def cycle_kernel(index, parts, ids, piece, table_ref, after, *refs):
    del after
    outs = refs[:parts]
    xh, xl, raw, table, made, sems = refs[parts:]
    peers, _, height, _ = piece.shape
    copies = fetch(
        [piece.at[j, index] for j in range(peers)] + [table_ref],
        [raw.at[j] for j in range(peers)] + [table],
        sems,
    )
    for j in range(peers):
        copies[j].wait()
        at = slice(j * height, (j + 1) * height)
        hi, lo = split(raw[j])
        xh[at, :] = hi
        xl[at, :] = lo
    copies[peers].wait()
    value = stacked3(table, xh[...], xl[...])
    block = outs[0].shape[0]
    for b in range(parts):
        made[jnp.bitwise_xor(ids[1], b)] = value[b * block : (b + 1) * block]
    sent = fetch([made.at[d] for d in range(parts)], outs, sems.at[pl.ds(peers + 1, parts)])
    for copy in sent:
        copy.wait()


def cycle_stage(index, ids, piece, table, parts, after):
    peers, _, height, width = piece.shape
    count = peers * height
    shape = jax.ShapeDtypeStruct((count // parts, width), F32)
    return pl.pallas_call(
        functools.partial(cycle_kernel, index, parts),
        out_shape=(shape,) * parts,
        in_specs=[SMEM] + [HBM] * 3,
        out_specs=(HBM,) * parts,
        scratch_shapes=[
            pltpu.VMEM((count, width), BF),
            pltpu.VMEM((count, width), BF),
            pltpu.VMEM((peers, height, width), F32),
            pltpu.VMEM(table.shape, BF),
            pltpu.VMEM((parts,) + shape.shape, F32),
            pltpu.SemaphoreType.DMA((peers + 1 + parts,)),
        ],
        compiler_params=params(24),
        cost_estimate=cost(0),
        name="cycle_stage",
    )(ids, piece, table, after)


def axial_kernel(mp, parts, ids, radial, cyc, axial, *refs):
    ins = refs[:parts]
    table_ref, after, out, x, xh, xl, raw, table, made, sems = refs[parts:]
    del after
    kc, width = ins[0].shape
    rows = width // mp
    half = mp * kc
    count = parts * rows
    copies = fetch([*ins, table_ref], [raw.at[j] for j in range(parts)] + [table], sems)
    for j in range(parts):
        source = jnp.bitwise_xor(ids[1], j)
        at = pl.ds(pl.multiple_of(source * rows, rows), rows)
        copies[j].wait()
        for m in range(mp):
            hi, lo = split(raw[j, :, m * rows : (m + 1) * rows])
            x[m * kc : (m + 1) * kc, at] = hi
            x[half + m * kc : half + (m + 1) * kc, at] = lo
    copies[parts].wait()
    mine = cyc[pl.ds(pl.multiple_of(ids[1] * kc, kc), kc), :]
    base = axial[...] + mine
    value = stacked3(x, table[0:count, :], table[count:, :])
    for m in range(mp):
        part = slice(m * kc, (m + 1) * kc)
        hi, lo = split(value[part] / (base + radial[ids[0] * mp + m]))
        xh[part, :] = hi
        xl[part, :] = lo
    made[...] = stacked3(table, xh[...], xl[...], True)
    copy = pltpu.make_async_copy(made, out, sems.at[parts + 1])
    copy.start()
    copy.wait()


def axial_stage(ids, radial, cyc, axial, pieces, table, mp, after):
    parts = len(pieces)
    kc, width = pieces[0].shape
    count = width // mp * parts
    return pl.pallas_call(
        functools.partial(axial_kernel, mp, parts),
        out_shape=jax.ShapeDtypeStruct((count, mp * kc), F32),
        in_specs=[SMEM, SMEM, VMEM, VMEM] + [HBM] * (parts + 2),
        out_specs=HBM,
        scratch_shapes=[
            pltpu.VMEM((2 * mp * kc, count), BF),
            pltpu.VMEM((mp * kc, count), BF),
            pltpu.VMEM((mp * kc, count), BF),
            pltpu.VMEM((parts, kc, width), F32),
            pltpu.VMEM(table.shape, BF),
            pltpu.VMEM((count, mp * kc), F32),
            pltpu.SemaphoreType.DMA((parts + 2,)),
        ],
        compiler_params=params(24),
        cost_estimate=cost(0),
        name="axial_stage",
    )(ids, radial, cyc, axial, *pieces, table, after)


def return_kernel(comp, mp, parts, peers, piece, *refs):
    out, x, y, raw, table, weave, kernel, made, sems = refs[-9:]
    _, few, width = piece.shape
    kc = width // mp
    count = table.shape[1]
    depth, span = kernel.shape[0] // 2, kernel.shape[1]
    half = mp * peers * few
    groups = count * mp // HALF
    copies = fetch((piece, *refs[:3]), (raw, table, weave, kernel), sems)
    copies[0].wait()
    for p in range(parts):
        for q in range(peers):
            for m in range(mp):
                row = (m * peers + q) * few
                hi, lo = split(raw[p * peers + q, :, m * kc : (m + 1) * kc])
                x[row : row + few, p * kc : (p + 1) * kc] = hi
                x[half + row : half + row + few, p * kc : (p + 1) * kc] = lo
    for copy in copies[1:]:
        copy.wait()
    value = split(stacked3(x, table[0:count, :], table[count:, :]))
    rows = peers * few
    front = iota((few, LANES), 1) < HALF
    for t in range(count // LANES):
        columns = slice(t * LANES, (t + 1) * LANES)
        for part, first in zip(value, (0, groups * few), strict=True):
            gathered = jnp.concatenate(
                [part[m * rows : (m + 1) * rows, columns] for m in range(mp)], axis=1
            )
            woven = dot(gathered, weave[...])
            for g in range(mp):
                block = woven[:, g * LANES : (g + 1) * LANES]
                turned = pltpu.roll(block, HALF, 1)
                row = first + 2 * (t * mp + g) * few
                for q in range(0, peers, 2):
                    one = slice(q * few, (q + 1) * few)
                    two = slice((q + 1) * few, (q + 2) * few)
                    to = slice(q * HALF, q * HALF + LANES)
                    y[row : row + few, to] = jnp.where(front, block[one], turned[two]).astype(BF)
                    y[row + few : row + 2 * few, to] = jnp.where(
                        front, turned[one], block[two]
                    ).astype(BF)
    result = stacked3(y, kernel[0:depth, :], kernel[depth:, :])
    for g in range(groups):
        made[:, g * span : (g + 1) * span] = result[g * few : (g + 1) * few, :]
    copy = pltpu.make_async_copy(made, out.at[comp], sems.at[4])
    copy.start()
    copy.wait()


def return_stage(comp, piece, table, weave, back, mp, parts, carried):
    devices, few, width = piece.shape
    peers = devices // parts
    count = table.shape[1]
    depth, span = back.shape[0] // 2, back.shape[1]
    groups = count * mp // HALF
    extra = [] if carried is None else [carried]
    return pl.pallas_call(
        functools.partial(return_kernel, comp, mp, parts, peers),
        out_shape=jax.ShapeDtypeStruct((3, few, groups * span), F32),
        in_specs=[HBM] * (4 + len(extra)),
        out_specs=HBM,
        scratch_shapes=[
            pltpu.VMEM((2 * mp * peers * few, count), BF),
            pltpu.VMEM((2 * groups * few, depth), BF),
            pltpu.VMEM(piece.shape, F32),
            pltpu.VMEM(table.shape, BF),
            pltpu.VMEM(weave.shape, BF),
            pltpu.VMEM(back.shape, BF),
            pltpu.VMEM((few, groups * span), F32),
            pltpu.SemaphoreType.DMA((5,)),
        ],
        input_output_aliases={4: 0} if extra else {},
        compiler_params=params(32),
        cost_estimate=cost(0),
        name="return_stage",
    )(piece, table, weave, back, *extra)


def across(block, axis):
    return lax.all_to_all(block, axis, split_axis=0, concat_axis=0, tiled=True)


def swap(pieces, axis):
    count = len(pieces)
    return [pieces[0]] + [
        lax.ppermute(pieces[d], axis, [(i, i ^ d) for i in range(count)]) for d in range(1, count)
    ]


ORDER = (
    ("stencil", (0,)),
    ("stencil", (1, 2)),
    ("cycle", 0),
    ("tables", None),
    ("axial", 0),
    ("cycle", 1),
    ("axial", 1),
    ("cycle", 2),
    ("return", 0),
    ("axial", 2),
    ("return", 1),
    ("return", 2),
)


def body(
    displace,
    load,
    history,
    stiffen,
    modulus,
    radial_slope,
    radial_basis,
    axial_eig,
    cycle_eig,
    radial_eig,
):
    parts = lax.axis_size("ax")
    peers = lax.axis_size("circ")
    mp = R // peers
    rows, flat = stiffen.shape
    count_a = parts * rows
    count_c = peers * flat // R
    me = lax.axis_index("circ").astype(jnp.int32)
    pe = lax.axis_index("ax").astype(jnp.int32)
    ids = jnp.stack([me, pe])

    upward, downward, leftward, rightward = pack(displace, history, stiffen)
    ahead = [(i, i + 1) for i in range(parts - 1)]
    back_ahead = [(j, i) for i, j in ahead]
    around = [(i, (i + 1) % peers) for i in range(peers)]
    back_around = [(j, i) for i, j in around]
    bottom = lax.ppermute(upward, "ax", back_ahead)
    top = lax.ppermute(downward, "ax", ahead)
    right = lax.ppermute(leftward, "circ", back_around)
    left = lax.ppermute(rightward, "circ", around)
    front = front_tables(radial_slope, radial_basis, mp)
    to_left, to_right = corners(top, bottom, front[0])
    right_corner = lax.ppermute(to_left, "circ", back_around)
    left_corner = lax.ppermute(to_right, "circ", around)
    halos = (top, bottom, left, left_corner, right, right_corner)

    cycle_table_stack = host_split(host_cycle(count_c))
    axial_table_stack = host_split(host_axial(count_a))
    weave = host_weave(mp)
    cyc = cycle_eig[:, None]
    axial = axial_eig[None, :]

    lines = [None] * 3
    out, after = None, ids
    for kind, i in ORDER:
        if kind == "stencil":
            after = stencil(
                i, mp, peers, modulus, displace, load, history, stiffen, halos, front, after
            )
            block = across(after, "circ")
            for index, comp in enumerate(i):
                lines[comp] = (index, block)
        elif kind == "tables":
            after = back = back_tables(radial_basis, mp, peers, after)
        elif kind == "cycle":
            index, block = lines[i]
            sent = cycle_stage(index, ids, block, cycle_table_stack, parts, after)
            after = sent[0]
            lines[i] = swap(list(sent), "ax")
        elif kind == "axial":
            after = axial_stage(
                ids, radial_eig, cyc, axial, lines[i], axial_table_stack, mp, after
            )
            block = after.reshape(parts * peers, rows // peers, -1)
            lines[i] = across(block, ("ax", "circ"))
        else:
            out = return_stage(i, lines[i], cycle_table_stack, weave, back, mp, parts, out)
            after = out
    return out


def tiled(mesh):
    parts, peers = mesh.shape["ax"], mesh.shape["circ"]
    rows, flat = NA // parts, NC // peers * R
    return (
        parts & (parts - 1) == 0
        and peers & (peers - 1) == 0
        and R == 32
        and R % peers == 0
        and peers * (R // peers) * 8 == 8 * R
        and rows % LANES == 0
        and (NC // parts) % LANES == 0
        and flat % (2 * LANES) == 0
        and (NC // peers) % 16 == 0
        and (rows // peers) % 16 == 0
        and HALF % (R // peers) == 0
        and peers % 2 == 0
    )


def solution(mesh):
    return jax.shard_map(
        body if tiled(mesh) else plain_body,
        mesh=mesh,
        in_specs=(
            P(None, "ax", "circ"),
            P(None, "ax", "circ"),
            P(None, "ax", "circ"),
            P("ax", "circ"),
            P(),
            P(),
            P(),
            P(),
            P(),
            P(),
        ),
        out_specs=P(None, ("ax", "circ"), None),
        check_vma=False,
    )
```

profile of v0, /device:TPU:0, one launch (start us, length us, event | category | flops | bytes accessed | tf_op | source)
XLA Modules:
  0.0 232.6 jit_solution(12402973910876957073)
XLA Ops:
  3.6 4.1 %collective-permute-start.4 = (f32[128,512]{1,0:T(8,128)}, f32[128,512]{1,0:T(8,128)S(1)}, u32[]{:S(2)}, u32[]{:S(2)}) collective-permute-start(f32[128,512]{1,0:T(8,128)} %get-tuple-element.34), channel_id=1, source_target_pairs={{1,0},{2,1},{3,2},{4,3},{5,4},{6,5},{7,6},{0,7},{9,8},{10,9},{11,1... | collective-permute-start | bytes 786440 | tf_op jit(solution)/shard_map/ppermute | solution.py:954
  7.7 3.8 %collective-permute-start = (f32[16,2048]{1,0:T(8,128)}, f32[16,2048]{1,0:T(8,128)S(1)}, u32[]{:S(2)}, u32[]{:S(2)}) collective-permute-start(f32[16,2048]{1,0:T(8,128)} %get-tuple-element.29), channel_id=1, source_target_pairs={{0,8},{8,16},{16,24},{1,9},{9,17},{17,25},{2,10},{10,18},{18,26},{... | collective-permute-start | bytes 393224 | tf_op jit(solution)/shard_map/ppermute | solution.py:953
  21.0 3.5 %collective-permute-start.5 = (f32[8,512]{1,0:T(8,128)}, f32[8,512]{1,0:T(8,128)S(1)}, u32[]{:S(2)}, u32[]{:S(2)}) collective-permute-start(f32[8,512]{1,0:T(8,128)} %get-tuple-element.35), channel_id=1, source_target_pairs={{1,0},{2,1},{3,2},{4,3},{5,4},{6,5},{7,6},{0,7},{9,8},{10,9},{11,1... | collective-permute-start | bytes 49160 | tf_op jit(solution)/shard_map/ppermute | solution.py:958
  27.0 13.6 %stencil.2.rest_6_ = f32[8,1,64,512]{3,2,1,0:T(8,128)} custom-call(f32[9,9]{1,0:T(8,128)} %modulus.3, f32[3,128,2048]{2,1,0:T(8,128)} %displace.5, f32[3,128,2048]{2,1,0:T(8,128)} %load.3, f32[9,128,2048]{2,1,0:T(8,128)} %history.5, f32[128,2048]{1,0:T(8,128)} %stiffen.5, f32[16,2048]{1,0:T(8,128)} %copy-done.18, f32[16,2048]{1,0:T(8,128)} %copy-done.19, ...), custom_call_target="tpu_custom_call" | custom-call | flops 1 | bytes 75600000 | tf_op jit(solution)/shard_map/stencil/pallas_call | solution.py:692
  40.6 4.8 %all-to-all-start.1 = ((f32[8,1,64,512]{3,2,1,0:T(8,128)}), f32[8,1,64,512]{3,2,1,0:T(8,128)}, u32[]{:S(2)}, u32[]{:S(2)}) async-start(f32[8,1,64,512]{3,2,1,0:T(8,128)} %stencil.2.rest_6_), calls=%async_computation.1 | async-start | bytes 2097152 | tf_op jit(solution)/shard_map/all_to_all | solution.py:899
  45.4 23.7 %stencil.3.after = f32[8,2,64,512]{3,2,1,0:T(8,128)} custom-call(f32[9,9]{1,0:T(8,128)} %modulus.3, f32[3,128,2048]{2,1,0:T(8,128)} %displace.5, f32[3,128,2048]{2,1,0:T(8,128)} %load.3, f32[9,128,2048]{2,1,0:T(8,128)} %history.5, f32[128,2048]{1,0:T(8,128)} %stiffen.5, f32[16,2048]{1,0:T(8,128)} %copy-done.18, f32[16,2048]{1,0:T(8,128)} %copy-done.19, ...), custom_call_target="tpu_custom_call" | custom-call | flops 1 | bytes 104400000 | tf_op jit(solution)/shard_map/stencil/pallas_call | solution.py:692
  72.1 4.3 %all-to-all-start = ((f32[8,2,64,512]{3,2,1,0:T(8,128)}), f32[8,2,64,512]{3,2,1,0:T(8,128)}, u32[]{:S(2)}, u32[]{:S(2)}) async-start(f32[8,2,64,512]{3,2,1,0:T(8,128)} %stencil.3.after), calls=%async_computation | async-start | bytes 4194304 | tf_op jit(solution)/shard_map/all_to_all | solution.py:899
  76.6 3.8 %cycle_stage.3 = (f32[128,512]{1,0:T(8,128)S(1)}, f32[128,512]{1,0:T(8,128)}, f32[128,512]{1,0:T(8,128)}, f32[128,512]{1,0:T(8,128)}) custom-call(s32[2]{0:T(128)S(1)} %copy-done.15, f32[8,1,64,512]{3,2,1,0:T(8,128)} %all-to-all-done.1.piece, bf16[1024,512]{1,0:T(8,128)(2,1)S(1)} %copy-done.1, f32[8,2,64,512]{3,2,1,0:T(8,128)S(1)} %copy-done.2), custom_call_target="tpu_custom_call" | custom-call | flops 1 | bytes 1 | tf_op jit(solution)/shard_map/cycle_stage/pallas_call | solution.py:745
  87.7 3.2 %collective-permute-done.6.refs_1_ = f32[128,512]{1,0:T(8,128)S(1)} collective-permute-done((f32[128,512]{1,0:T(8,128)}, f32[128,512]{1,0:T(8,128)S(1)}, u32[]{:S(2)}, u32[]{:S(2)}) %collective-permute-start.6) | collective-permute-done | bytes 262176 | tf_op jit(solution)/shard_map/ppermute | solution.py:905
  90.9 6.8 %collective-permute-done.7.refs_2_ = f32[128,512]{1,0:T(8,128)S(1)} collective-permute-done((f32[128,512]{1,0:T(8,128)}, f32[128,512]{1,0:T(8,128)S(1)}, u32[]{:S(2)}, u32[]{:S(2)}) %collective-permute-start.7) | collective-permute-done | bytes 262176 | tf_op jit(solution)/shard_map/ppermute | solution.py:905
  99.8 3.8 %axial_stage.3.after = f32[512,512]{1,0:T(8,128)} custom-call(s32[2]{0:T(128)S(1)} %copy-done.15, f32[32]{0:T(128)S(1)} %copy-done.17, f32[512,1]{1,0:T(8,128)S(1)} %copy.18.cyc, f32[1,512]{1,0:T(1,128)S(1)} %bitcast.9, f32[128,512]{1,0:T(8,128)S(1)} %copy-done.13, f32[128,512]{1,0:T(8,128)S(1)} %collective-permute-done.6.refs_1_, ...), custom_call_target="tpu_custom_call" | custom-call | flops 1 | bytes 1 | tf_op jit(solution)/shard_map/axial_stage/pallas_call | solution.py:800
  103.7 21.9 %all-to-all-done.piece = f32[8,2,64,512]{3,2,1,0:T(8,128)} async-done(((f32[8,2,64,512]{3,2,1,0:T(8,128)}), f32[8,2,64,512]{3,2,1,0:T(8,128)}, u32[]{:S(2)}, u32[]{:S(2)}) %all-to-all-start) | async-done | bytes 2097184 | tf_op jit(solution)/shard_map/all_to_all | solution.py:899
  125.6 3.6 %all-to-all-start.2 = ((f32[32,16,512]{2,1,0:T(8,128)}), f32[32,16,512]{2,1,0:T(8,128)}, u32[]{:S(2)}, u32[]{:S(2)}) async-start(f32[32,16,512]{2,1,0:T(8,128)} %bitcast.4), calls=%async_computation.2 | async-start | bytes 2097152 | tf_op jit(solution)/shard_map/all_to_all | solution.py:899
  135.8 10.7 %collective-permute-done.9.refs_1_ = f32[128,512]{1,0:T(8,128)S(1)} collective-permute-done((f32[128,512]{1,0:T(8,128)S(1)}, f32[128,512]{1,0:T(8,128)S(1)}, u32[]{:S(2)}, u32[]{:S(2)}) %collective-permute-start.9) | collective-permute-done | bytes 262176 | tf_op jit(solution)/shard_map/ppermute | solution.py:905
  147.5 7.1 %collective-permute-done.11.refs_3_ = f32[128,512]{1,0:T(8,128)S(1)} collective-permute-done((f32[128,512]{1,0:T(8,128)S(1)}, f32[128,512]{1,0:T(8,128)S(1)}, u32[]{:S(2)}, u32[]{:S(2)}) %collective-permute-start.11) | collective-permute-done | bytes 262176 | tf_op jit(solution)/shard_map/ppermute | solution.py:905
  158.5 5.3 %all-to-all-start.4 = ((f32[32,16,512]{2,1,0:T(8,128)}), f32[32,16,512]{2,1,0:T(8,128)}, u32[]{:S(2)}, u32[]{:S(2)}) async-start(f32[32,16,512]{2,1,0:T(8,128)} %bitcast.7), calls=%async_computation.4 | async-start | bytes 2097152 | tf_op jit(solution)/shard_map/all_to_all | solution.py:899
  171.6 4.8 %return_stage.3.refs_5_.refs_3_ = f32[3,16,16384]{2,1,0:T(8,128)} custom-call(f32[32,16,512]{2,1,0:T(8,128)} %all-to-all-done.2.piece, bf16[1024,512]{1,0:T(8,128)(2,1)S(1)} %copy-done.1, bf16[512,512]{1,0:T(8,128)(2,1)S(1)} %copy-done.7, bf16[1024,512]{1,0:T(8,128)(2,1)S(1)} %back_tables.1.refs_5_.refs_2_), custom_call_target="tpu_custom_call" | custom-call | flops 1 | bytes 1 | tf_op jit(solution)/shard_map/return_stage/pallas_call | solution.py:876
  176.5 4.6 %collective-permute-done.12.refs_1_ = f32[128,512]{1,0:T(8,128)S(1)} collective-permute-done((f32[128,512]{1,0:T(8,128)S(1)}, f32[128,512]{1,0:T(8,128)S(1)}, u32[]{:S(2)}, u32[]{:S(2)}) %collective-permute-start.12) | collective-permute-done | bytes 262176 | tf_op jit(solution)/shard_map/ppermute | solution.py:905
  181.1 4.7 %collective-permute-done.13.refs_2_ = f32[128,512]{1,0:T(8,128)S(1)} collective-permute-done((f32[128,512]{1,0:T(8,128)S(1)}, f32[128,512]{1,0:T(8,128)S(1)}, u32[]{:S(2)}, u32[]{:S(2)}) %collective-permute-start.13) | collective-permute-done | bytes 262176 | tf_op jit(solution)/shard_map/ppermute | solution.py:905
  185.8 3.2 %collective-permute-done.14.refs_3_ = f32[128,512]{1,0:T(8,128)S(1)} collective-permute-done((f32[128,512]{1,0:T(8,128)S(1)}, f32[128,512]{1,0:T(8,128)S(1)}, u32[]{:S(2)}, u32[]{:S(2)}) %collective-permute-start.14) | collective-permute-done | bytes 262176 | tf_op jit(solution)/shard_map/ppermute | solution.py:905
  194.8 5.1 %all-to-all-start.3 = ((f32[32,16,512]{2,1,0:T(8,128)}), f32[32,16,512]{2,1,0:T(8,128)}, u32[]{:S(2)}, u32[]{:S(2)}) async-start(f32[32,16,512]{2,1,0:T(8,128)} %bitcast.8), calls=%async_computation.3 | async-start | bytes 2097152 | tf_op jit(solution)/shard_map/all_to_all | solution.py:899
  201.0 4.9 %return_stage.4.refs_3_ = f32[3,16,16384]{2,1,0:T(8,128)} custom-call(f32[32,16,512]{2,1,0:T(8,128)} %all-to-all-done.4.piece, bf16[1024,512]{1,0:T(8,128)(2,1)S(1)} %copy-done.1, bf16[512,512]{1,0:T(8,128)(2,1)S(1)} %copy-done.8, bf16[1024,512]{1,0:T(8,128)(2,1)S(1)} %back_tables.1.refs_5_.refs_2_, ...), custom_call_target="tpu_custom_call", output_to_operand_aliasing={{}: (4, {})} | custom-call | flops 1 | bytes 1 | tf_op jit(solution)/shard_map/return_stage/pallas_call | solution.py:876
  205.9 21.6 %all-to-all-done.3.piece = f32[32,16,512]{2,1,0:T(8,128)} async-done(((f32[32,16,512]{2,1,0:T(8,128)}), f32[32,16,512]{2,1,0:T(8,128)}, u32[]{:S(2)}, u32[]{:S(2)}) %all-to-all-start.3) | async-done | bytes 1048608 | tf_op jit(solution)/shard_map/all_to_all | solution.py:899
  227.6 4.8 %return_stage.5 = f32[3,16,16384]{2,1,0:T(8,128)} custom-call(f32[32,16,512]{2,1,0:T(8,128)} %all-to-all-done.3.piece, bf16[1024,512]{1,0:T(8,128)(2,1)S(1)} %copy-done.1, bf16[512,512]{1,0:T(8,128)(2,1)S(1)} %copy-done.9, bf16[1024,512]{1,0:T(8,128)(2,1)S(1)} %back_tables.1.refs_5_.refs_2_, ...), custom_call_target="tpu_custom_call", output_to_operand_aliasing={{}: (4, {})} | custom-call | flops 1 | bytes 1 | tf_op jit(solution)/shard_map/return_stage/pallas_call | solution.py:876
  (83 shorter events, 54.1 us)
Async XLA Ops:
  3.1 23.0 %collective-permute-start.2 = (f32[128,512]{1,0:T(8,128)}, f32[128,512]{1,0:T(8,128)S(1)}, u32[]{:S(2)}, u32[]{:S(2)}) collective-permute-start(f32[128,512]{1,0:T(8,128)} %get-tuple-element.31), channel_id=1, source_target_pairs={{0,1},{1,2},{2,3},{3,4},{4,5},{5,6},{6,7},{7,0},{8,9},{9,10},{10,1... | collective-permute-start | bytes 786440 | tf_op jit(solution)/shard_map/ppermute | solution.py:955
  3.6 22.5 %collective-permute-start.4 = (f32[128,512]{1,0:T(8,128)}, f32[128,512]{1,0:T(8,128)S(1)}, u32[]{:S(2)}, u32[]{:S(2)}) collective-permute-start(f32[128,512]{1,0:T(8,128)} %get-tuple-element.34), channel_id=1, source_target_pairs={{1,0},{2,1},{3,2},{4,3},{5,4},{6,5},{7,6},{0,7},{9,8},{10,9},{11,1... | collective-permute-start | bytes 786440 | tf_op jit(solution)/shard_map/ppermute | solution.py:954
  7.7 8.0 %collective-permute-start = (f32[16,2048]{1,0:T(8,128)}, f32[16,2048]{1,0:T(8,128)S(1)}, u32[]{:S(2)}, u32[]{:S(2)}) collective-permute-start(f32[16,2048]{1,0:T(8,128)} %get-tuple-element.29), channel_id=1, source_target_pairs={{0,8},{8,16},{16,24},{1,9},{9,17},{17,25},{2,10},{10,18},{18,26},{... | collective-permute-start | bytes 393224 | tf_op jit(solution)/shard_map/ppermute | solution.py:953
  11.6 7.1 %collective-permute-start.1 = (f32[16,2048]{1,0:T(8,128)}, f32[16,2048]{1,0:T(8,128)S(1)}, u32[]{:S(2)}, u32[]{:S(2)}) collective-permute-start(f32[16,2048]{1,0:T(8,128)} %get-tuple-element.30), channel_id=1, source_target_pairs={{8,0},{16,8},{24,16},{9,1},{17,9},{25,17},{10,2},{18,10},{26,18},{... | collective-permute-start | bytes 393224 | tf_op jit(solution)/shard_map/ppermute | solution.py:952
  21.0 5.2 %collective-permute-start.3 = (f32[8,512]{1,0:T(8,128)}, f32[8,512]{1,0:T(8,128)S(1)}, u32[]{:S(2)}, u32[]{:S(2)}) collective-permute-start(f32[8,512]{1,0:T(8,128)} %get-tuple-element.33), channel_id=1, source_target_pairs={{0,1},{1,2},{2,3},{3,4},{4,5},{5,6},{6,7},{7,0},{8,9},{9,10},{10,1... | collective-permute-start | bytes 49160 | tf_op jit(solution)/shard_map/ppermute | solution.py:959
  21.0 5.2 %collective-permute-start.5 = (f32[8,512]{1,0:T(8,128)}, f32[8,512]{1,0:T(8,128)S(1)}, u32[]{:S(2)}, u32[]{:S(2)}) collective-permute-start(f32[8,512]{1,0:T(8,128)} %get-tuple-element.35), channel_id=1, source_target_pairs={{1,0},{2,1},{3,2},{4,3},{5,4},{6,5},{7,6},{0,7},{9,8},{10,9},{11,1... | collective-permute-start | bytes 49160 | tf_op jit(solution)/shard_map/ppermute | solution.py:958
  40.6 31.5 %all-to-all-start.1 = ((f32[8,1,64,512]{3,2,1,0:T(8,128)}), f32[8,1,64,512]{3,2,1,0:T(8,128)}, u32[]{:S(2)}, u32[]{:S(2)}) async-start(f32[8,1,64,512]{3,2,1,0:T(8,128)} %stencil.2.rest_6_), calls=%async_computation.1 | async-start | bytes 2097152 | tf_op jit(solution)/shard_map/all_to_all | solution.py:899
  72.1 53.4 %all-to-all-start = ((f32[8,2,64,512]{3,2,1,0:T(8,128)}), f32[8,2,64,512]{3,2,1,0:T(8,128)}, u32[]{:S(2)}, u32[]{:S(2)}) async-start(f32[8,2,64,512]{3,2,1,0:T(8,128)} %stencil.3.after), calls=%async_computation | async-start | bytes 4194304 | tf_op jit(solution)/shard_map/all_to_all | solution.py:899
  76.5 21.1 %copy-start.16 = (f32[512]{0:T(512)S(1)}, f32[512]{0:T(512)}, u32[]{:S(2)}) copy-start(f32[512]{0:T(512)} %param.20) | copy-start | bytes 6148
  76.6 21.1 %copy-start.17 = (f32[32]{0:T(128)S(1)}, f32[32]{0:T(128)}, u32[]{:S(2)}) copy-start(f32[32]{0:T(128)} %radial.5) | copy-start | bytes 388
  81.1 9.8 %collective-permute-start.6 = (f32[128,512]{1,0:T(8,128)}, f32[128,512]{1,0:T(8,128)S(1)}, u32[]{:S(2)}, u32[]{:S(2)}) collective-permute-start(f32[128,512]{1,0:T(8,128)} %get-tuple-element.42), channel_id=1, source_target_pairs={{0,8},{8,0},{16,24},{24,16},{1,9},{9,1},{17,25},{25,17},{2,10},{10... | collective-permute-start | bytes 786440 | tf_op jit(solution)/shard_map/ppermute | solution.py:905
  83.5 14.1 %collective-permute-start.7 = (f32[128,512]{1,0:T(8,128)}, f32[128,512]{1,0:T(8,128)S(1)}, u32[]{:S(2)}, u32[]{:S(2)}) collective-permute-start(f32[128,512]{1,0:T(8,128)} %get-tuple-element.43), channel_id=1, source_target_pairs={{0,16},{8,24},{16,0},{24,8},{1,17},{9,25},{17,1},{25,9},{2,18},{10... | collective-permute-start | bytes 786440 | tf_op jit(solution)/shard_map/ppermute | solution.py:905
  83.5 14.1 %collective-permute-start.8 = (f32[128,512]{1,0:T(8,128)}, f32[128,512]{1,0:T(8,128)S(1)}, u32[]{:S(2)}, u32[]{:S(2)}) collective-permute-start(f32[128,512]{1,0:T(8,128)} %get-tuple-element.44), channel_id=1, source_target_pairs={{0,24},{8,16},{16,8},{24,0},{1,25},{9,17},{17,9},{25,1},{2,26},{10... | collective-permute-start | bytes 786440 | tf_op jit(solution)/shard_map/ppermute | solution.py:905
  125.6 29.0 %copy-start.4 = (bf16[1024,512]{1,0:T(8,128)(2,1)S(1)}, bf16[1024,512]{1,0:T(8,128)(2,1)}, u32[]{:S(2)}) copy-start(bf16[1024,512]{1,0:T(8,128)(2,1)} %constant.15.clone.refs_4_) | copy-start | bytes 3145732
  125.6 32.9 %all-to-all-start.2 = ((f32[32,16,512]{2,1,0:T(8,128)}), f32[32,16,512]{2,1,0:T(8,128)}, u32[]{:S(2)}, u32[]{:S(2)}) async-start(f32[32,16,512]{2,1,0:T(8,128)} %bitcast.4), calls=%async_computation.2 | async-start | bytes 2097152 | tf_op jit(solution)/shard_map/all_to_all | solution.py:899
  132.1 14.3 %collective-permute-start.9 = (f32[128,512]{1,0:T(8,128)S(1)}, f32[128,512]{1,0:T(8,128)S(1)}, u32[]{:S(2)}, u32[]{:S(2)}) collective-permute-start(f32[128,512]{1,0:T(8,128)S(1)} %get-tuple-element.46), channel_id=1, source_target_pairs={{0,8},{8,0},{16,24},{24,16},{1,9},{9,1},{17,25},{25,17},{2,10},{10... | collective-permute-start | bytes 786440 | tf_op jit(solution)/shard_map/ppermute | solution.py:905
  134.3 13.2 %collective-permute-start.10 = (f32[128,512]{1,0:T(8,128)S(1)}, f32[128,512]{1,0:T(8,128)S(1)}, u32[]{:S(2)}, u32[]{:S(2)}) collective-permute-start(f32[128,512]{1,0:T(8,128)S(1)} %get-tuple-element.47), channel_id=1, source_target_pairs={{0,16},{8,24},{16,0},{24,8},{1,17},{9,25},{17,1},{25,9},{2,18},{10... | collective-permute-start | bytes 786440 | tf_op jit(solution)/shard_map/ppermute | solution.py:905
  135.4 19.2 %collective-permute-start.11 = (f32[128,512]{1,0:T(8,128)S(1)}, f32[128,512]{1,0:T(8,128)S(1)}, u32[]{:S(2)}, u32[]{:S(2)}) collective-permute-start(f32[128,512]{1,0:T(8,128)S(1)} %get-tuple-element.48), channel_id=1, source_target_pairs={{0,24},{8,16},{16,8},{24,0},{1,25},{9,17},{17,9},{25,1},{2,26},{10... | collective-permute-start | bytes 786440 | tf_op jit(solution)/shard_map/ppermute | solution.py:905
  158.5 36.4 %all-to-all-start.4 = ((f32[32,16,512]{2,1,0:T(8,128)}), f32[32,16,512]{2,1,0:T(8,128)}, u32[]{:S(2)}, u32[]{:S(2)}) async-start(f32[32,16,512]{2,1,0:T(8,128)} %bitcast.7), calls=%async_computation.4 | async-start | bytes 2097152 | tf_op jit(solution)/shard_map/all_to_all | solution.py:899
  168.1 13.0 %collective-permute-start.12 = (f32[128,512]{1,0:T(8,128)S(1)}, f32[128,512]{1,0:T(8,128)S(1)}, u32[]{:S(2)}, u32[]{:S(2)}) collective-permute-start(f32[128,512]{1,0:T(8,128)S(1)} %get-tuple-element.50), channel_id=1, source_target_pairs={{0,8},{8,0},{16,24},{24,16},{1,9},{9,1},{17,25},{25,17},{2,10},{10... | collective-permute-start | bytes 786440 | tf_op jit(solution)/shard_map/ppermute | solution.py:905
  169.6 16.2 %collective-permute-start.13 = (f32[128,512]{1,0:T(8,128)S(1)}, f32[128,512]{1,0:T(8,128)S(1)}, u32[]{:S(2)}, u32[]{:S(2)}) collective-permute-start(f32[128,512]{1,0:T(8,128)S(1)} %get-tuple-element.51), channel_id=1, source_target_pairs={{0,16},{8,24},{16,0},{24,8},{1,17},{9,25},{17,1},{25,9},{2,18},{10... | collective-permute-start | bytes 786440 | tf_op jit(solution)/shard_map/ppermute | solution.py:905
  171.1 17.9 %collective-permute-start.14 = (f32[128,512]{1,0:T(8,128)S(1)}, f32[128,512]{1,0:T(8,128)S(1)}, u32[]{:S(2)}, u32[]{:S(2)}) collective-permute-start(f32[128,512]{1,0:T(8,128)S(1)} %get-tuple-element.52), channel_id=1, source_target_pairs={{0,24},{8,16},{16,8},{24,0},{1,25},{9,17},{17,9},{25,1},{2,26},{10... | collective-permute-start | bytes 786440 | tf_op jit(solution)/shard_map/ppermute | solution.py:905
  194.8 32.7 %all-to-all-start.3 = ((f32[32,16,512]{2,1,0:T(8,128)}), f32[32,16,512]{2,1,0:T(8,128)}, u32[]{:S(2)}, u32[]{:S(2)}) async-start(f32[32,16,512]{2,1,0:T(8,128)} %bitcast.8), calls=%async_computation.3 | async-start | bytes 2097152 | tf_op jit(solution)/shard_map/all_to_all | solution.py:899
  201.0 26.5 %copy-start.9 = (bf16[512,512]{1,0:T(8,128)(2,1)S(1)}, bf16[512,512]{1,0:T(8,128)(2,1)}, u32[]{:S(2)}) copy-start(bf16[512,512]{1,0:T(8,128)(2,1)} %constant.16.clone.refs_1_) | copy-start | bytes 1572868
  (21 other events, 61.9 us)
where the time goes:
time: 234 us; the launch traced here: 233 us
  waiting for transfers between devices  91.5 us (39%)
  Pallas kernels  80.8 us (35%)
  starting transfers between devices  47.5 us (20%)
  local copies, waits for them, and re-layouts  11.6 us (5%)
    all_to_all x5, waiting for transfers between devices, across(): return lax.all_to_all(block, axis, split_axis=0, concat_axis=0, tiled=True)  46.5 us
    ppermute x9, waiting for transfers between devices, swap(): lax.ppermute(pieces[d], axis, [(i, i ^ d) for i in range(count)])  41.2 us
    pallas_call x2, Pallas kernels, stencil(): pl.pallas_call(functools.partial(stencil_kernel, comps, mp, peers), out_s...  37.3 us
    all_to_all x5, starting transfers between devices, across(): return lax.all_to_all(block, axis, split_axis=0, concat_axis=0, tiled=True)  23.1 us
    pallas_call x3, Pallas kernels, return_stage(): pl.pallas_call(functools.partial(return_kernel, comp, mp, parts, peers),...  14.6 us
    unnamed x50, local copies, waits for them, and re-layouts  11.5 us
    ppermute x9, starting transfers between devices, swap(): lax.ppermute(pieces[d], axis, [(i, i ^ d) for i in range(count)])  11.1 us
    pallas_call x3, Pallas kernels, cycle_stage(): pl.pallas_call(functools.partial(cycle_kernel, index, parts), out_shape=(...  9.84 us
  transfers between devices with their start and end apart: 20, of which 13 were waited for; matrix products, arithmetic and copies ran while one was open for 0% of the time, Pallas kernels for 25%

commit v1 on v0

--- a/solution.py
+++ b/solution.py
@@ -476,7 +476,8 @@
     *rest,
 ):
     n = len(comps)
-    out, xd, hx, sx, ld, st, sums, diffs, made, krh, krl, kbh, kbl, kwh, kwl, sems = rest[7:]
+    outs = rest[7 : 7 + n]
+    xd, hx, sx, ld, st, sums, diffs, made, krh, krl, kbh, kbl, kwh, kwl, sems = rest[7 + n :]
     rows, flat = stiffen.shape
     tall = rows + HALO
     tiles = flat // LANES
@@ -676,7 +677,7 @@
             lax.fori_loop(0, tiles // 2, message_step, 0, unroll=True)
         else:
             lax.fori_loop(0, tiles // 4, message_pair, 0)
-        sent += [pltpu.make_async_copy(message, out.at[:, index], sems.at[base + 1 + 4 * n + index])]
+        sent += [pltpu.make_async_copy(message, outs[index], sems.at[base + 1 + 4 * n + index])]
         sent[-1].start()
     for copy in sent:
         copy.wait()
@@ -691,9 +692,9 @@
     block = (flat // R, mp * rows)
     return pl.pallas_call(
         functools.partial(stencil_kernel, comps, mp, peers),
-        out_shape=jax.ShapeDtypeStruct((peers, n) + block, F32),
+        out_shape=(jax.ShapeDtypeStruct((peers,) + block, F32),) * n,
         in_specs=[SMEM] + [HBM] * 4 + [VMEM] * 6 + [HBM] * 7,
-        out_specs=HBM,
+        out_specs=(HBM,) * n,
         scratch_shapes=[
             pltpu.VMEM((3, tiles + 1, PAD + tall + HALO, LANES), F32),
             pltpu.VMEM((3 * n, tall, wide), F32),
@@ -712,13 +713,13 @@
     )(modulus, displace, load, history, stiffen, *halos, *tables, after)
 
 
-def cycle_kernel(index, parts, ids, piece, table_ref, after, *refs):
+def cycle_kernel(parts, ids, piece, table_ref, after, *refs):
     del after
     outs = refs[:parts]
     xh, xl, raw, table, made, sems = refs[parts:]
-    peers, _, height, _ = piece.shape
+    peers, height, _ = piece.shape
     copies = fetch(
-        [piece.at[j, index] for j in range(peers)] + [table_ref],
+        [piece.at[j] for j in range(peers)] + [table_ref],
         [raw.at[j] for j in range(peers)] + [table],
         sems,
     )
@@ -738,12 +739,12 @@
         copy.wait()
 
 
-def cycle_stage(index, ids, piece, table, parts, after):
-    peers, _, height, width = piece.shape
+def cycle_stage(ids, piece, table, parts, after):
+    peers, height, width = piece.shape
     count = peers * height
     shape = jax.ShapeDtypeStruct((count // parts, width), F32)
     return pl.pallas_call(
-        functools.partial(cycle_kernel, index, parts),
+        functools.partial(cycle_kernel, parts),
         out_shape=(shape,) * parts,
         in_specs=[SMEM] + [HBM] * 3,
         out_specs=(HBM,) * parts,
@@ -761,10 +762,10 @@
     )(ids, piece, table, after)
 
 
-def axial_kernel(mp, parts, ids, radial, cyc, axial, *refs):
+def axial_kernel(slot, mp, parts, ids, radial, cyc, axial, *refs):
     ins = refs[:parts]
-    table_ref, after, out, x, xh, xl, raw, table, made, sems = refs[parts:]
-    del after
+    table_ref = refs[parts]
+    out, x, xh, xl, raw, table, made, sems = refs[-8:]
     kc, width = ins[0].shape
     rows = width // mp
     half = mp * kc
@@ -787,20 +788,21 @@
         hi, lo = split(value[part] / (base + radial[ids[0] * mp + m]))
         xh[part, :] = hi
         xl[part, :] = lo
-    made[...] = stacked3(table, xh[...], xl[...], True)
-    copy = pltpu.make_async_copy(made, out, sems.at[parts + 1])
+    made[...] = stacked3(table, xh[...], xl[...], True).reshape(made.shape)
+    copy = pltpu.make_async_copy(made, out.at[:, slot], sems.at[parts + 1])
     copy.start()
     copy.wait()
 
 
-def axial_stage(ids, radial, cyc, axial, pieces, table, mp, after):
+def axial_stage(slot, slots, ids, radial, cyc, axial, pieces, table, mp, devices, after, carried):
     parts = len(pieces)
     kc, width = pieces[0].shape
     count = width // mp * parts
+    extra = [] if carried is None else [carried]
     return pl.pallas_call(
-        functools.partial(axial_kernel, mp, parts),
-        out_shape=jax.ShapeDtypeStruct((count, mp * kc), F32),
-        in_specs=[SMEM, SMEM, VMEM, VMEM] + [HBM] * (parts + 2),
+        functools.partial(axial_kernel, slot, mp, parts),
+        out_shape=jax.ShapeDtypeStruct((devices, slots, count // devices, mp * kc), F32),
+        in_specs=[SMEM, SMEM, VMEM, VMEM] + [HBM] * (parts + 2 + len(extra)),
         out_specs=HBM,
         scratch_shapes=[
             pltpu.VMEM((2 * mp * kc, count), BF),
@@ -808,24 +810,25 @@
             pltpu.VMEM((mp * kc, count), BF),
             pltpu.VMEM((parts, kc, width), F32),
             pltpu.VMEM(table.shape, BF),
-            pltpu.VMEM((count, mp * kc), F32),
+            pltpu.VMEM((devices, count // devices, mp * kc), F32),
             pltpu.SemaphoreType.DMA((parts + 2,)),
         ],
+        input_output_aliases={parts + 6: 0} if extra else {},
         compiler_params=params(24),
         cost_estimate=cost(0),
         name="axial_stage",
-    )(ids, radial, cyc, axial, *pieces, table, after)
-
-
-def return_kernel(comp, mp, parts, peers, piece, *refs):
+    )(ids, radial, cyc, axial, *pieces, table, after, *extra)
+
+
+def return_kernel(slot, comp, mp, parts, peers, piece, *refs):
     out, x, y, raw, table, weave, kernel, made, sems = refs[-9:]
-    _, few, width = piece.shape
+    _, _, few, width = piece.shape
     kc = width // mp
     count = table.shape[1]
     depth, span = kernel.shape[0] // 2, kernel.shape[1]
     half = mp * peers * few
     groups = count * mp // HALF
-    copies = fetch((piece, *refs[:3]), (raw, table, weave, kernel), sems)
+    copies = fetch((piece.at[:, slot], *refs[:3]), (raw, table, weave, kernel), sems)
     copies[0].wait()
     for p in range(parts):
         for q in range(peers):
@@ -866,22 +869,22 @@
     copy.wait()
 
 
-def return_stage(comp, piece, table, weave, back, mp, parts, carried):
-    devices, few, width = piece.shape
+def return_stage(slot, comp, piece, table, weave, back, mp, parts, carried):
+    devices, _, few, width = piece.shape
     peers = devices // parts
     count = table.shape[1]
     depth, span = back.shape[0] // 2, back.shape[1]
     groups = count * mp // HALF
     extra = [] if carried is None else [carried]
     return pl.pallas_call(
-        functools.partial(return_kernel, comp, mp, parts, peers),
+        functools.partial(return_kernel, slot, comp, mp, parts, peers),
         out_shape=jax.ShapeDtypeStruct((3, few, groups * span), F32),
         in_specs=[HBM] * (4 + len(extra)),
         out_specs=HBM,
         scratch_shapes=[
             pltpu.VMEM((2 * mp * peers * few, count), BF),
             pltpu.VMEM((2 * groups * few, depth), BF),
-            pltpu.VMEM(piece.shape, F32),
+            pltpu.VMEM((devices, few, width), F32),
             pltpu.VMEM(table.shape, BF),
             pltpu.VMEM(weave.shape, BF),
             pltpu.VMEM(back.shape, BF),
@@ -895,6 +898,23 @@
     )(piece, table, weave, back, *extra)
 
 
+def gate_kernel(block, after, out):
+    del block, after, out
+
+
+def gate(block, after):
+    return pl.pallas_call(
+        gate_kernel,
+        out_shape=jax.ShapeDtypeStruct(block.shape, block.dtype),
+        in_specs=[HBM, HBM],
+        out_specs=HBM,
+        input_output_aliases={0: 0},
+        compiler_params=params(),
+        cost_estimate=cost(0),
+        name="gate",
+    )(block, after)
+
+
 def across(block, axis):
     return lax.all_to_all(block, axis, split_axis=0, concat_axis=0, tiled=True)
 
@@ -908,15 +928,20 @@
 
 ORDER = (
     ("stencil", (0,)),
+    ("forward", 0),
     ("stencil", (1, 2)),
+    ("forward", 1),
     ("cycle", 0),
     ("tables", None),
     ("axial", 0),
+    ("forward", 2),
     ("cycle", 1),
     ("axial", 1),
+    ("backward", (0, 1)),
     ("cycle", 2),
+    ("axial", 2),
+    ("backward", (2,)),
     ("return", 0),
-    ("axial", 2),
     ("return", 1),
     ("return", 2),
 )
@@ -966,30 +991,46 @@
     axial = axial_eig[None, :]
 
     lines = [None] * 3
-    out, after = None, ids
+    out, after, solved = None, ids, None
     for kind, i in ORDER:
         if kind == "stencil":
-            after = stencil(
+            blocks = stencil(
                 i, mp, peers, modulus, displace, load, history, stiffen, halos, front, after
             )
-            block = across(after, "circ")
-            for index, comp in enumerate(i):
-                lines[comp] = (index, block)
+            after = blocks[0]
+            for comp, block in zip(i, blocks, strict=True):
+                lines[comp] = block
+        elif kind == "forward":
+            lines[i] = across(lines[i] if i < 2 else gate(lines[i], after), "circ")
         elif kind == "tables":
             after = back = back_tables(radial_basis, mp, peers, after)
         elif kind == "cycle":
-            index, block = lines[i]
-            sent = cycle_stage(index, ids, block, cycle_table_stack, parts, after)
+            sent = cycle_stage(ids, lines[i], cycle_table_stack, parts, after)
             after = sent[0]
             lines[i] = swap(list(sent), "ax")
         elif kind == "axial":
-            after = axial_stage(
-                ids, radial_eig, cyc, axial, lines[i], axial_table_stack, mp, after
+            slot, slots = (i, 2) if i < 2 else (0, 1)
+            solved = after = axial_stage(
+                slot,
+                slots,
+                ids,
+                radial_eig,
+                cyc,
+                axial,
+                lines[i],
+                axial_table_stack,
+                mp,
+                parts * peers,
+                after,
+                solved if slot else None,
             )
-            block = after.reshape(parts * peers, rows // peers, -1)
-            lines[i] = across(block, ("ax", "circ"))
+        elif kind == "backward":
+            block = across(solved, ("ax", "circ"))
+            for slot, comp in enumerate(i):
+                lines[comp] = (slot, block)
         else:
-            out = return_stage(i, lines[i], cycle_table_stack, weave, back, mp, parts, out)
+            slot, block = lines[i]
+            out = return_stage(slot, i, block, cycle_table_stack, weave, back, mp, parts, out)
             after = out
     return out
 

time: 234 us -> 227 us (0.970)
  local copies, waits for them, and re-layouts: 11.6 us -> 7.45 us
  waiting for transfers between devices: 91.5 us -> 89.1 us
    all_to_all x5, waiting for transfers between devices: 46.5 us -> 36 us  [across(): return lax.all_to_all(block, axis, split_axis=0, concat_axis=0, tiled=True)]
    ppermute x9, waiting for transfers between devices: 41.2 us -> 49.2 us  [swap(): lax.ppermute(pieces[d], axis, [(i, i ^ d) for i in range(count)])]
    unnamed x50 -> x40, local copies, waits for them, and re-layouts: 11.5 us -> 7.31 us
    pallas_call x9 -> x10, Pallas kernels: 34.1 us -> 36.1 us  [the longest x3 14.6 us: return_stage(): pl.pallas_call(functools.partial(return_kernel, slot, comp, mp, parts, pe...]
  transfers between devices with their start and end apart: 20 -> 20, of which waited for: 13 -> 12; matrix products, arithmetic and copies ran while one was open for 0% -> 0% of each run, Pallas kernels for 25% -> 27%
where the time goes in v1:
time: 227 us; the launch traced here: 226 us
  waiting for transfers between devices  89.1 us (39%)
  Pallas kernels  82.8 us (36%)
  starting transfers between devices  45.3 us (20%)
  local copies, waits for them, and re-layouts  7.45 us (3%)
    ppermute x9, waiting for transfers between devices, swap(): lax.ppermute(pieces[d], axis, [(i, i ^ d) for i in range(count)])  49.2 us
    pallas_call x2, Pallas kernels, stencil(): pl.pallas_call(functools.partial(stencil_kernel, comps, mp, peers), out_s...  37.4 us
    all_to_all x5, waiting for transfers between devices, across(): return lax.all_to_all(block, axis, split_axis=0, concat_axis=0, tiled=True)  36 us
    all_to_all x5, starting transfers between devices, across(): return lax.all_to_all(block, axis, split_axis=0, concat_axis=0, tiled=True)  21 us
    pallas_call x3, Pallas kernels, return_stage(): pl.pallas_call(functools.partial(return_kernel, slot, comp, mp, parts, pe...  14.6 us
    pallas_call x3, Pallas kernels, axial_stage(): pl.pallas_call(functools.partial(axial_kernel, slot, mp, parts), out_shap...  11.4 us
    ppermute x9, starting transfers between devices, swap(): lax.ppermute(pieces[d], axis, [(i, i ^ d) for i in range(count)])  11 us
    pallas_call x3, Pallas kernels, cycle_stage(): pl.pallas_call(functools.partial(cycle_kernel, parts), out_shape=(shape,)...  10.1 us
  transfers between devices with their start and end apart: 20, of which 12 were waited for; matrix products, arithmetic and copies ran while one was open for 0% of the time, Pallas kernels for 27%

profile of v1, /device:TPU:0, one launch (start us, length us, event | category | flops | bytes accessed | tf_op | source)
XLA Modules:
  0.0 225.8 jit_solution(748142486897559707)
XLA Ops:
  3.6 4.1 %collective-permute-start.4 = (f32[128,512]{1,0:T(8,128)}, f32[128,512]{1,0:T(8,128)S(1)}, u32[]{:S(2)}, u32[]{:S(2)}) collective-permute-start(f32[128,512]{1,0:T(8,128)} %get-tuple-element.36), channel_id=1, source_target_pairs={{1,0},{2,1},{3,2},{4,3},{5,4},{6,5},{7,6},{0,7},{9,8},{10,9},{11,1... | collective-permute-start | bytes 786440 | tf_op jit(solution)/shard_map/ppermute | solution.py:979
  7.7 3.8 %collective-permute-start = (f32[16,2048]{1,0:T(8,128)}, f32[16,2048]{1,0:T(8,128)S(1)}, u32[]{:S(2)}, u32[]{:S(2)}) collective-permute-start(f32[16,2048]{1,0:T(8,128)} %get-tuple-element.31), channel_id=1, source_target_pairs={{0,8},{8,16},{16,24},{1,9},{9,17},{17,25},{2,10},{10,18},{18,26},{... | collective-permute-start | bytes 393224 | tf_op jit(solution)/shard_map/ppermute | solution.py:978
  21.0 3.5 %collective-permute-start.5 = (f32[8,512]{1,0:T(8,128)}, f32[8,512]{1,0:T(8,128)S(1)}, u32[]{:S(2)}, u32[]{:S(2)}) collective-permute-start(f32[8,512]{1,0:T(8,128)} %get-tuple-element.37), channel_id=1, source_target_pairs={{1,0},{2,1},{3,2},{4,3},{5,4},{6,5},{7,6},{0,7},{9,8},{10,9},{11,1... | collective-permute-start | bytes 49160 | tf_op jit(solution)/shard_map/ppermute | solution.py:983
  27.0 13.6 %stencil.2.rest_6_ = f32[8,64,512]{2,1,0:T(8,128)} custom-call(f32[9,9]{1,0:T(8,128)} %modulus.3, f32[3,128,2048]{2,1,0:T(8,128)} %displace.5, f32[3,128,2048]{2,1,0:T(8,128)} %load.3, f32[9,128,2048]{2,1,0:T(8,128)} %history.5, f32[128,2048]{1,0:T(8,128)} %stiffen.5, f32[16,2048]{1,0:T(8,128)} %copy-done.13, f32[16,2048]{1,0:T(8,128)} %copy-done.14, ...), custom_call_target="tpu_custom_call" | custom-call | flops 1 | bytes 75600000 | tf_op jit(solution)/shard_map/stencil/pallas_call | solution.py:693
  40.6 4.8 %all-to-all-start = ((f32[8,64,512]{2,1,0:T(8,128)}), f32[8,64,512]{2,1,0:T(8,128)S(1)}, u32[]{:S(2)}, u32[]{:S(2)}) async-start(f32[8,64,512]{2,1,0:T(8,128)} %stencil.2.rest_6_), calls=%async_computation | async-start | bytes 2097152 | tf_op jit(solution)/shard_map/all_to_all | solution.py:919
  45.4 23.8 %stencil.3 = (f32[8,64,512]{2,1,0:T(8,128)}, f32[8,64,512]{2,1,0:T(8,128)}) custom-call(f32[9,9]{1,0:T(8,128)} %modulus.3, f32[3,128,2048]{2,1,0:T(8,128)} %displace.5, f32[3,128,2048]{2,1,0:T(8,128)} %load.3, f32[9,128,2048]{2,1,0:T(8,128)} %history.5, f32[128,2048]{1,0:T(8,128)} %stiffen.5, f32[16,2048]{1,0:T(8,128)} %copy-done.13, f32[16,2048]{1,0:T(8,128)} %copy-done.14, ...), custom_call_target="tpu_custom_call" | custom-call | flops 1 | bytes 104400000 | tf_op jit(solution)/shard_map/stencil/pallas_call | solution.py:693
  72.0 4.4 %all-to-all-start.2 = ((f32[8,64,512]{2,1,0:T(8,128)}), f32[8,64,512]{2,1,0:T(8,128)}, u32[]{:S(2)}, u32[]{:S(2)}) async-start(f32[8,64,512]{2,1,0:T(8,128)} %get-tuple-element.44.after), calls=%async_computation.2 | async-start | bytes 2097152 | tf_op jit(solution)/shard_map/all_to_all | solution.py:919
  77.7 4.1 %cycle_stage.3 = (f32[128,512]{1,0:T(8,128)S(1)}, f32[128,512]{1,0:T(8,128)}, f32[128,512]{1,0:T(8,128)}, f32[128,512]{1,0:T(8,128)}) custom-call(s32[2]{0:T(128)S(1)} %copy-done.10, f32[8,64,512]{2,1,0:T(8,128)S(1)} %all-to-all-done.piece, bf16[1024,512]{1,0:T(8,128)(2,1)S(1)} %copy-done, f32[8,64,512]{2,1,0:T(8,128)S(1)} %copy-done.4), custom_call_target="tpu_custom_call" | custom-call | flops 1 | bytes 1 | tf_op jit(solution)/shard_map/cycle_stage/pallas_call | solution.py:746
  92.3 6.8 %collective-permute-done.7.refs_2_ = f32[128,512]{1,0:T(8,128)} collective-permute-done((f32[128,512]{1,0:T(8,128)}, f32[128,512]{1,0:T(8,128)}, u32[]{:S(2)}, u32[]{:S(2)}) %collective-permute-start.7) | collective-permute-done | bytes 262176 | tf_op jit(solution)/shard_map/ppermute | solution.py:925
  100.1 4.7 %axial_stage.3.after.refs_6_ = f32[32,2,16,512]{3,2,1,0:T(8,128)} custom-call(s32[2]{0:T(128)S(1)} %copy-done.10, f32[32]{0:T(128)S(1)} %copy-done.12, f32[512,1]{1,0:T(8,128)S(1)} %copy.20.cyc, f32[1,512]{1,0:T(1,128)S(1)} %bitcast.4, f32[128,512]{1,0:T(8,128)S(1)} %copy-done.8, f32[128,512]{1,0:T(8,128)} %collective-permute-done.6.refs_1_, ...), custom_call_target="tpu_custom_call" | custom-call | flops 1 | bytes 1 | tf_op jit(solution)/shard_map/axial_stage/pallas_call | solution.py:802
  104.8 4.8 %all-to-all-start.1 = ((f32[8,64,512]{2,1,0:T(8,128)}), f32[8,64,512]{2,1,0:T(8,128)}, u32[]{:S(2)}, u32[]{:S(2)}) async-start(f32[8,64,512]{2,1,0:T(8,128)} %gate.1), calls=%async_computation.1 | async-start | bytes 2097152 | tf_op jit(solution)/shard_map/all_to_all | solution.py:919
  116.1 5.6 %collective-permute-done.9.refs_1_ = f32[128,512]{1,0:T(8,128)S(1)} collective-permute-done((f32[128,512]{1,0:T(8,128)S(1)}, f32[128,512]{1,0:T(8,128)S(1)}, u32[]{:S(2)}, u32[]{:S(2)}) %collective-permute-start.9) | collective-permute-done | bytes 262176 | tf_op jit(solution)/shard_map/ppermute | solution.py:925
  121.7 5.3 %collective-permute-done.10.refs_2_ = f32[128,512]{1,0:T(8,128)S(1)} collective-permute-done((f32[128,512]{1,0:T(8,128)S(1)}, f32[128,512]{1,0:T(8,128)S(1)}, u32[]{:S(2)}, u32[]{:S(2)}) %collective-permute-start.10) | collective-permute-done | bytes 262176 | tf_op jit(solution)/shard_map/ppermute | solution.py:925
  127.0 3.8 %axial_stage.4.after = f32[32,2,16,512]{3,2,1,0:T(8,128)} custom-call(s32[2]{0:T(128)S(1)} %copy-done.10, f32[32]{0:T(128)S(1)} %copy-done.12, f32[512,1]{1,0:T(8,128)S(1)} %copy.20.cyc, f32[1,512]{1,0:T(1,128)S(1)} %bitcast.5, f32[128,512]{1,0:T(8,128)S(1)} %get-tuple-element.49.refs_0_.refs_5_, ...), custom_call_target="tpu_custom_call", output_to_operand_aliasing={{}: (10, {})} | custom-call | flops 1 | bytes 1 | tf_op jit(solution)/shard_map/axial_stage/pallas_call | solution.py:802
  130.9 5.4 %all-to-all-done.1.piece = f32[8,64,512]{2,1,0:T(8,128)} async-done(((f32[8,64,512]{2,1,0:T(8,128)}), f32[8,64,512]{2,1,0:T(8,128)}, u32[]{:S(2)}, u32[]{:S(2)}) %all-to-all-start.1) | async-done | bytes 1048608 | tf_op jit(solution)/shard_map/all_to_all | solution.py:919
  136.2 3.7 %all-to-all-start.4 = ((f32[32,2,16,512]{3,2,1,0:T(8,128)}), f32[32,2,16,512]{3,2,1,0:T(8,128)}, u32[]{:S(2)}, u32[]{:S(2)}) async-start(f32[32,2,16,512]{3,2,1,0:T(8,128)} %axial_stage.4.after), calls=%async_computation.4 | async-start | bytes 4194304 | tf_op jit(solution)/shard_map/all_to_all | solution.py:919
  146.5 17.7 %collective-permute-done.12.refs_1_ = f32[128,512]{1,0:T(8,128)S(1)} collective-permute-done((f32[128,512]{1,0:T(8,128)S(1)}, f32[128,512]{1,0:T(8,128)S(1)}, u32[]{:S(2)}, u32[]{:S(2)}) %collective-permute-start.12) | collective-permute-done | bytes 262176 | tf_op jit(solution)/shard_map/ppermute | solution.py:925
  164.2 10.6 %collective-permute-done.14.refs_3_ = f32[128,512]{1,0:T(8,128)S(1)} collective-permute-done((f32[128,512]{1,0:T(8,128)S(1)}, f32[128,512]{1,0:T(8,128)S(1)}, u32[]{:S(2)}, u32[]{:S(2)}) %collective-permute-start.14) | collective-permute-done | bytes 262176 | tf_op jit(solution)/shard_map/ppermute | solution.py:925
  178.7 11.1 %all-to-all-done.4.piece = f32[32,2,16,512]{3,2,1,0:T(8,128)} async-done(((f32[32,2,16,512]{3,2,1,0:T(8,128)}), f32[32,2,16,512]{3,2,1,0:T(8,128)}, u32[]{:S(2)}, u32[]{:S(2)}) %all-to-all-start.4) | async-done | bytes 2097184 | tf_op jit(solution)/shard_map/all_to_all | solution.py:919
  189.8 3.4 %all-to-all-start.3 = ((f32[32,1,16,512]{3,2,1,0:T(8,128)}), f32[32,1,16,512]{3,2,1,0:T(8,128)}, u32[]{:S(2)}, u32[]{:S(2)}) async-start(f32[32,1,16,512]{3,2,1,0:T(8,128)} %copy-done.5), calls=%async_computation.3 | async-start | bytes 2097152 | tf_op jit(solution)/shard_map/all_to_all | solution.py:919
  194.2 4.8 %return_stage.3.refs_3_ = f32[3,16,16384]{2,1,0:T(8,128)} custom-call(f32[32,2,16,512]{3,2,1,0:T(8,128)} %all-to-all-done.4.piece, bf16[1024,512]{1,0:T(8,128)(2,1)S(1)} %copy-done, bf16[512,512]{1,0:T(8,128)(2,1)S(1)} %copy-done.2, bf16[1024,512]{1,0:T(8,128)(2,1)S(1)} %back_tables.1.refs_5_.refs_2_), custom_call_target="tpu_custom_call" | custom-call | flops 1 | bytes 1 | tf_op jit(solution)/shard_map/return_stage/pallas_call | solution.py:879
  199.1 4.9 %return_stage.4.refs_3_ = f32[3,16,16384]{2,1,0:T(8,128)} custom-call(f32[32,2,16,512]{3,2,1,0:T(8,128)} %all-to-all-done.4.piece, bf16[1024,512]{1,0:T(8,128)(2,1)S(1)} %copy-done, bf16[512,512]{1,0:T(8,128)(2,1)S(1)} %copy-done.2, bf16[1024,512]{1,0:T(8,128)(2,1)S(1)} %back_tables.1.refs_5_.refs_2_, ...), custom_call_target="tpu_custom_call", output_to_operand_aliasing={{}: (4, {})} | custom-call | flops 1 | bytes 1 | tf_op jit(solution)/shard_map/return_stage/pallas_call | solution.py:879
  204.0 16.7 %all-to-all-done.3.piece = f32[32,1,16,512]{3,2,1,0:T(8,128)} async-done(((f32[32,1,16,512]{3,2,1,0:T(8,128)}), f32[32,1,16,512]{3,2,1,0:T(8,128)}, u32[]{:S(2)}, u32[]{:S(2)}) %all-to-all-start.3) | async-done | bytes 1048608 | tf_op jit(solution)/shard_map/all_to_all | solution.py:919
  220.8 4.8 %return_stage.5 = f32[3,16,16384]{2,1,0:T(8,128)} custom-call(f32[32,1,16,512]{3,2,1,0:T(8,128)} %all-to-all-done.3.piece, bf16[1024,512]{1,0:T(8,128)(2,1)S(1)} %copy-done, bf16[512,512]{1,0:T(8,128)(2,1)S(1)} %copy-done.3, bf16[1024,512]{1,0:T(8,128)(2,1)S(1)} %back_tables.1.refs_5_.refs_2_, ...), custom_call_target="tpu_custom_call", output_to_operand_aliasing={{}: (4, {})} | custom-call | flops 1 | bytes 1 | tf_op jit(solution)/shard_map/return_stage/pallas_call | solution.py:879
  (74 shorter events, 49.0 us)
Async XLA Ops:
  3.1 23.1 %collective-permute-start.2 = (f32[128,512]{1,0:T(8,128)}, f32[128,512]{1,0:T(8,128)S(1)}, u32[]{:S(2)}, u32[]{:S(2)}) collective-permute-start(f32[128,512]{1,0:T(8,128)} %get-tuple-element.33), channel_id=1, source_target_pairs={{0,1},{1,2},{2,3},{3,4},{4,5},{5,6},{6,7},{7,0},{8,9},{9,10},{10,1... | collective-permute-start | bytes 786440 | tf_op jit(solution)/shard_map/ppermute | solution.py:980
  3.6 22.6 %collective-permute-start.4 = (f32[128,512]{1,0:T(8,128)}, f32[128,512]{1,0:T(8,128)S(1)}, u32[]{:S(2)}, u32[]{:S(2)}) collective-permute-start(f32[128,512]{1,0:T(8,128)} %get-tuple-element.36), channel_id=1, source_target_pairs={{1,0},{2,1},{3,2},{4,3},{5,4},{6,5},{7,6},{0,7},{9,8},{10,9},{11,1... | collective-permute-start | bytes 786440 | tf_op jit(solution)/shard_map/ppermute | solution.py:979
  7.7 8.0 %collective-permute-start = (f32[16,2048]{1,0:T(8,128)}, f32[16,2048]{1,0:T(8,128)S(1)}, u32[]{:S(2)}, u32[]{:S(2)}) collective-permute-start(f32[16,2048]{1,0:T(8,128)} %get-tuple-element.31), channel_id=1, source_target_pairs={{0,8},{8,16},{16,24},{1,9},{9,17},{17,25},{2,10},{10,18},{18,26},{... | collective-permute-start | bytes 393224 | tf_op jit(solution)/shard_map/ppermute | solution.py:978
  11.6 7.1 %collective-permute-start.1 = (f32[16,2048]{1,0:T(8,128)}, f32[16,2048]{1,0:T(8,128)S(1)}, u32[]{:S(2)}, u32[]{:S(2)}) collective-permute-start(f32[16,2048]{1,0:T(8,128)} %get-tuple-element.32), channel_id=1, source_target_pairs={{8,0},{16,8},{24,16},{9,1},{17,9},{25,17},{10,2},{18,10},{26,18},{... | collective-permute-start | bytes 393224 | tf_op jit(solution)/shard_map/ppermute | solution.py:977
  21.0 5.2 %collective-permute-start.3 = (f32[8,512]{1,0:T(8,128)}, f32[8,512]{1,0:T(8,128)S(1)}, u32[]{:S(2)}, u32[]{:S(2)}) collective-permute-start(f32[8,512]{1,0:T(8,128)} %get-tuple-element.35), channel_id=1, source_target_pairs={{0,1},{1,2},{2,3},{3,4},{4,5},{5,6},{6,7},{7,0},{8,9},{9,10},{10,1... | collective-permute-start | bytes 49160 | tf_op jit(solution)/shard_map/ppermute | solution.py:984
  21.0 5.2 %collective-permute-start.5 = (f32[8,512]{1,0:T(8,128)}, f32[8,512]{1,0:T(8,128)S(1)}, u32[]{:S(2)}, u32[]{:S(2)}) collective-permute-start(f32[8,512]{1,0:T(8,128)} %get-tuple-element.37), channel_id=1, source_target_pairs={{1,0},{2,1},{3,2},{4,3},{5,4},{6,5},{7,6},{0,7},{9,8},{10,9},{11,1... | collective-permute-start | bytes 49160 | tf_op jit(solution)/shard_map/ppermute | solution.py:983
  40.6 31.4 %all-to-all-start = ((f32[8,64,512]{2,1,0:T(8,128)}), f32[8,64,512]{2,1,0:T(8,128)S(1)}, u32[]{:S(2)}, u32[]{:S(2)}) async-start(f32[8,64,512]{2,1,0:T(8,128)} %stencil.2.rest_6_), calls=%async_computation | async-start | bytes 2097152 | tf_op jit(solution)/shard_map/all_to_all | solution.py:919
  45.4 31.0 %copy-start = (bf16[1024,512]{1,0:T(8,128)(2,1)S(1)}, bf16[1024,512]{1,0:T(8,128)(2,1)}, u32[]{:S(2)}) copy-start(bf16[1024,512]{1,0:T(8,128)(2,1)} %constant.14.clone.table_ref.refs_0_) | copy-start | bytes 3145732
  45.4 31.0 %copy-start.10 = (s32[2]{0:T(128)S(1)}, s32[2]{0:T(128)}, u32[]{:S(2)}) copy-start(s32[2]{0:T(128)} %pad_add_fusion.rest_6_.ids) | copy-start | bytes 28
  72.0 27.1 %copy-start.11 = (f32[512]{0:T(512)S(1)}, f32[512]{0:T(512)}, u32[]{:S(2)}) copy-start(f32[512]{0:T(512)} %param.20) | copy-start | bytes 6148
  72.0 27.1 %copy-start.12 = (f32[32]{0:T(128)S(1)}, f32[32]{0:T(128)}, u32[]{:S(2)}) copy-start(f32[32]{0:T(128)} %radial.5) | copy-start | bytes 388
  72.0 32.7 %all-to-all-start.2 = ((f32[8,64,512]{2,1,0:T(8,128)}), f32[8,64,512]{2,1,0:T(8,128)}, u32[]{:S(2)}, u32[]{:S(2)}) async-start(f32[8,64,512]{2,1,0:T(8,128)} %get-tuple-element.44.after), calls=%async_computation.2 | async-start | bytes 2097152 | tf_op jit(solution)/shard_map/all_to_all | solution.py:919
  82.5 9.9 %collective-permute-start.6 = (f32[128,512]{1,0:T(8,128)}, f32[128,512]{1,0:T(8,128)}, u32[]{:S(2)}, u32[]{:S(2)}) collective-permute-start(f32[128,512]{1,0:T(8,128)} %get-tuple-element.46), channel_id=1, source_target_pairs={{0,8},{8,0},{16,24},{24,16},{1,9},{9,1},{17,25},{25,17},{2,10},{10... | collective-permute-start | bytes 786440 | tf_op jit(solution)/shard_map/ppermute | solution.py:925
  84.9 14.2 %collective-permute-start.7 = (f32[128,512]{1,0:T(8,128)}, f32[128,512]{1,0:T(8,128)}, u32[]{:S(2)}, u32[]{:S(2)}) collective-permute-start(f32[128,512]{1,0:T(8,128)} %get-tuple-element.47), channel_id=1, source_target_pairs={{0,16},{8,24},{16,0},{24,8},{1,17},{9,25},{17,1},{25,9},{2,18},{10... | collective-permute-start | bytes 786440 | tf_op jit(solution)/shard_map/ppermute | solution.py:925
  84.9 14.2 %collective-permute-start.8 = (f32[128,512]{1,0:T(8,128)}, f32[128,512]{1,0:T(8,128)}, u32[]{:S(2)}, u32[]{:S(2)}) collective-permute-start(f32[128,512]{1,0:T(8,128)} %get-tuple-element.48), channel_id=1, source_target_pairs={{0,24},{8,16},{16,8},{24,0},{1,25},{9,17},{17,9},{25,1},{2,26},{10... | collective-permute-start | bytes 786440 | tf_op jit(solution)/shard_map/ppermute | solution.py:925
  104.8 31.5 %all-to-all-start.1 = ((f32[8,64,512]{2,1,0:T(8,128)}), f32[8,64,512]{2,1,0:T(8,128)}, u32[]{:S(2)}, u32[]{:S(2)}) async-start(f32[8,64,512]{2,1,0:T(8,128)} %gate.1), calls=%async_computation.1 | async-start | bytes 2097152 | tf_op jit(solution)/shard_map/all_to_all | solution.py:919
  112.5 9.2 %collective-permute-start.9 = (f32[128,512]{1,0:T(8,128)S(1)}, f32[128,512]{1,0:T(8,128)S(1)}, u32[]{:S(2)}, u32[]{:S(2)}) collective-permute-start(f32[128,512]{1,0:T(8,128)S(1)} %get-tuple-element.50), channel_id=1, source_target_pairs={{0,8},{8,0},{16,24},{24,16},{1,9},{9,1},{17,25},{25,17},{2,10},{10... | collective-permute-start | bytes 786440 | tf_op jit(solution)/shard_map/ppermute | solution.py:925
  112.9 14.1 %collective-permute-start.10 = (f32[128,512]{1,0:T(8,128)S(1)}, f32[128,512]{1,0:T(8,128)S(1)}, u32[]{:S(2)}, u32[]{:S(2)}) collective-permute-start(f32[128,512]{1,0:T(8,128)S(1)} %get-tuple-element.51), channel_id=1, source_target_pairs={{0,16},{8,24},{16,0},{24,8},{1,17},{9,25},{17,1},{25,9},{2,18},{10... | collective-permute-start | bytes 786440 | tf_op jit(solution)/shard_map/ppermute | solution.py:925
  114.4 12.7 %collective-permute-start.11 = (f32[128,512]{1,0:T(8,128)S(1)}, f32[128,512]{1,0:T(8,128)S(1)}, u32[]{:S(2)}, u32[]{:S(2)}) collective-permute-start(f32[128,512]{1,0:T(8,128)S(1)} %get-tuple-element.52), channel_id=1, source_target_pairs={{0,24},{8,16},{16,8},{24,0},{1,25},{9,17},{17,9},{25,1},{2,26},{10... | collective-permute-start | bytes 786440 | tf_op jit(solution)/shard_map/ppermute | solution.py:925
  136.2 53.6 %all-to-all-start.4 = ((f32[32,2,16,512]{3,2,1,0:T(8,128)}), f32[32,2,16,512]{3,2,1,0:T(8,128)}, u32[]{:S(2)}, u32[]{:S(2)}) async-start(f32[32,2,16,512]{3,2,1,0:T(8,128)} %axial_stage.4.after), calls=%async_computation.4 | async-start | bytes 4194304 | tf_op jit(solution)/shard_map/all_to_all | solution.py:919
  143.0 21.2 %collective-permute-start.12 = (f32[128,512]{1,0:T(8,128)S(1)}, f32[128,512]{1,0:T(8,128)S(1)}, u32[]{:S(2)}, u32[]{:S(2)}) collective-permute-start(f32[128,512]{1,0:T(8,128)S(1)} %get-tuple-element.54), channel_id=1, source_target_pairs={{0,8},{8,0},{16,24},{24,16},{1,9},{9,1},{17,25},{25,17},{2,10},{10... | collective-permute-start | bytes 786440 | tf_op jit(solution)/shard_map/ppermute | solution.py:925
  144.4 19.8 %collective-permute-start.13 = (f32[128,512]{1,0:T(8,128)S(1)}, f32[128,512]{1,0:T(8,128)S(1)}, u32[]{:S(2)}, u32[]{:S(2)}) collective-permute-start(f32[128,512]{1,0:T(8,128)S(1)} %get-tuple-element.55), channel_id=1, source_target_pairs={{0,16},{8,24},{16,0},{24,8},{1,17},{9,25},{17,1},{25,9},{2,18},{10... | collective-permute-start | bytes 786440 | tf_op jit(solution)/shard_map/ppermute | solution.py:925
  145.9 28.9 %collective-permute-start.14 = (f32[128,512]{1,0:T(8,128)S(1)}, f32[128,512]{1,0:T(8,128)S(1)}, u32[]{:S(2)}, u32[]{:S(2)}) collective-permute-start(f32[128,512]{1,0:T(8,128)S(1)} %get-tuple-element.56), channel_id=1, source_target_pairs={{0,24},{8,16},{16,8},{24,0},{1,25},{9,17},{17,9},{25,1},{2,26},{10... | collective-permute-start | bytes 786440 | tf_op jit(solution)/shard_map/ppermute | solution.py:925
  189.8 30.9 %all-to-all-start.3 = ((f32[32,1,16,512]{3,2,1,0:T(8,128)}), f32[32,1,16,512]{3,2,1,0:T(8,128)}, u32[]{:S(2)}, u32[]{:S(2)}) async-start(f32[32,1,16,512]{3,2,1,0:T(8,128)} %copy-done.5), calls=%async_computation.3 | async-start | bytes 2097152 | tf_op jit(solution)/shard_map/all_to_all | solution.py:919
  (16 other events, 95.2 us)

commit v2 on v1

--- a/solution.py
+++ b/solution.py
@@ -898,21 +898,21 @@
     )(piece, table, weave, back, *extra)
 
 
-def gate_kernel(block, after, out):
-    del block, after, out
-
-
-def gate(block, after):
+def gate_kernel(*refs):
+    del refs
+
+
+def gate(block, *after):
     return pl.pallas_call(
         gate_kernel,
         out_shape=jax.ShapeDtypeStruct(block.shape, block.dtype),
-        in_specs=[HBM, HBM],
+        in_specs=[HBM] * (1 + len(after)),
         out_specs=HBM,
         input_output_aliases={0: 0},
-        compiler_params=params(),
+        compiler_params=params(16),
         cost_estimate=cost(0),
         name="gate",
-    )(block, after)
+    )(block, *after)
 
 
 def across(block, axis):
@@ -933,8 +933,8 @@
     ("forward", 1),
     ("cycle", 0),
     ("tables", None),
+    ("forward", 2),
     ("axial", 0),
-    ("forward", 2),
     ("cycle", 1),
     ("axial", 1),
     ("backward", (0, 1)),
@@ -1001,7 +1001,7 @@
             for comp, block in zip(i, blocks, strict=True):
                 lines[comp] = block
         elif kind == "forward":
-            lines[i] = across(lines[i] if i < 2 else gate(lines[i], after), "circ")
+            lines[i] = across(lines[i] if i < 2 else gate(lines[i], *lines[0][1:]), "circ")
         elif kind == "tables":
             after = back = back_tables(radial_basis, mp, peers, after)
         elif kind == "cycle":

time: 227 us -> 232 us (1.022)
  local copies, waits for them, and re-layouts: 7.45 us -> 13.4 us
    unnamed x40 -> x60, local copies, waits for them, and re-layouts: 7.31 us -> 13.2 us
    ppermute x9, waiting for transfers between devices: 49.2 us -> 53.1 us  [swap(): lax.ppermute(pieces[d], axis, [(i, i ^ d) for i in range(count)])]
    all_to_all x5, waiting for transfers between devices: 36 us -> 32.4 us  [across(): return lax.all_to_all(block, axis, split_axis=0, concat_axis=0, tiled=True)]
  transfers between devices with their start and end apart: 20 -> 20, of which waited for: 12 -> 12; matrix products, arithmetic and copies ran while one was open for 0% -> 0% of each run, Pallas kernels for 27% -> 26%
where the time goes in v2:
time: 232 us; the launch traced here: 231 us
  waiting for transfers between devices  89.4 us (39%)
  Pallas kernels  81.5 us (35%)
  starting transfers between devices  45.5 us (20%)
  local copies, waits for them, and re-layouts  13.4 us (6%)
    ppermute x9, waiting for transfers between devices, swap(): lax.ppermute(pieces[d], axis, [(i, i ^ d) for i in range(count)])  53.1 us
    pallas_call x2, Pallas kernels, stencil(): pl.pallas_call(functools.partial(stencil_kernel, comps, mp, peers), out_s...  37.4 us
    all_to_all x5, waiting for transfers between devices, across(): return lax.all_to_all(block, axis, split_axis=0, concat_axis=0, tiled=True)  32.4 us
    all_to_all x5, starting transfers between devices, across(): return lax.all_to_all(block, axis, split_axis=0, concat_axis=0, tiled=True)  20.8 us
    pallas_call x3, Pallas kernels, return_stage(): pl.pallas_call(functools.partial(return_kernel, slot, comp, mp, parts, pe...  14.6 us
    unnamed x60, local copies, waits for them, and re-layouts  13.2 us
    ppermute x9, starting transfers between devices, swap(): lax.ppermute(pieces[d], axis, [(i, i ^ d) for i in range(count)])  11.4 us
    pallas_call x3, Pallas kernels, axial_stage(): pl.pallas_call(functools.partial(axial_kernel, slot, mp, parts), out_shap...  10.6 us
  transfers between devices with their start and end apart: 20, of which 12 were waited for; matrix products, arithmetic and copies ran while one was open for 0% of the time, Pallas kernels for 26%

profile of v2, /device:TPU:0, one launch (start us, length us, event | category | flops | bytes accessed | tf_op | source)
XLA Modules:
  0.0 230.9 jit_solution(4176223327454550890)
XLA Ops:
  3.7 4.1 %collective-permute-start.4 = (f32[128,512]{1,0:T(8,128)}, f32[128,512]{1,0:T(8,128)S(1)}, u32[]{:S(2)}, u32[]{:S(2)}) collective-permute-start(f32[128,512]{1,0:T(8,128)} %get-tuple-element.36), channel_id=1, source_target_pairs={{1,0},{2,1},{3,2},{4,3},{5,4},{6,5},{7,6},{0,7},{9,8},{10,9},{11,1... | collective-permute-start | bytes 786440 | tf_op jit(solution)/shard_map/ppermute | solution.py:979
  7.8 3.8 %collective-permute-start = (f32[16,2048]{1,0:T(8,128)}, f32[16,2048]{1,0:T(8,128)S(1)}, u32[]{:S(2)}, u32[]{:S(2)}) collective-permute-start(f32[16,2048]{1,0:T(8,128)} %get-tuple-element.31), channel_id=1, source_target_pairs={{0,8},{8,16},{16,24},{1,9},{9,17},{17,25},{2,10},{10,18},{18,26},{... | collective-permute-start | bytes 393224 | tf_op jit(solution)/shard_map/ppermute | solution.py:978
  21.0 3.5 %collective-permute-start.5 = (f32[8,512]{1,0:T(8,128)}, f32[8,512]{1,0:T(8,128)S(1)}, u32[]{:S(2)}, u32[]{:S(2)}) collective-permute-start(f32[8,512]{1,0:T(8,128)} %get-tuple-element.37), channel_id=1, source_target_pairs={{1,0},{2,1},{3,2},{4,3},{5,4},{6,5},{7,6},{0,7},{9,8},{10,9},{11,1... | collective-permute-start | bytes 49160 | tf_op jit(solution)/shard_map/ppermute | solution.py:983
  27.0 13.6 %stencil.2.rest_6_ = f32[8,64,512]{2,1,0:T(8,128)} custom-call(f32[9,9]{1,0:T(8,128)} %modulus.3, f32[3,128,2048]{2,1,0:T(8,128)} %displace.5, f32[3,128,2048]{2,1,0:T(8,128)} %load.3, f32[9,128,2048]{2,1,0:T(8,128)} %history.5, f32[128,2048]{1,0:T(8,128)} %stiffen.5, f32[16,2048]{1,0:T(8,128)} %copy-done.23, f32[16,2048]{1,0:T(8,128)} %copy-done.24, ...), custom_call_target="tpu_custom_call" | custom-call | flops 1 | bytes 75600000 | tf_op jit(solution)/shard_map/stencil/pallas_call | solution.py:693
  40.6 4.8 %all-to-all-start = ((f32[8,64,512]{2,1,0:T(8,128)}), f32[8,64,512]{2,1,0:T(8,128)S(1)}, u32[]{:S(2)}, u32[]{:S(2)}) async-start(f32[8,64,512]{2,1,0:T(8,128)} %stencil.2.rest_6_), calls=%async_computation | async-start | bytes 2097152 | tf_op jit(solution)/shard_map/all_to_all | solution.py:919
  45.4 23.8 %stencil.3 = (f32[8,64,512]{2,1,0:T(8,128)}, f32[8,64,512]{2,1,0:T(8,128)}) custom-call(f32[9,9]{1,0:T(8,128)} %modulus.3, f32[3,128,2048]{2,1,0:T(8,128)} %displace.5, f32[3,128,2048]{2,1,0:T(8,128)} %load.3, f32[9,128,2048]{2,1,0:T(8,128)} %history.5, f32[128,2048]{1,0:T(8,128)} %stiffen.5, f32[16,2048]{1,0:T(8,128)} %copy-done.23, f32[16,2048]{1,0:T(8,128)} %copy-done.24, ...), custom_call_target="tpu_custom_call" | custom-call | flops 1 | bytes 104400000 | tf_op jit(solution)/shard_map/stencil/pallas_call | solution.py:693
  72.0 3.6 %all-to-all-start.2 = ((f32[8,64,512]{2,1,0:T(8,128)}), f32[8,64,512]{2,1,0:T(8,128)S(1)}, u32[]{:S(2)}, u32[]{:S(2)}) async-start(f32[8,64,512]{2,1,0:T(8,128)} %get-tuple-element.44.after), calls=%async_computation.2 | async-start | bytes 2097152 | tf_op jit(solution)/shard_map/all_to_all | solution.py:919
  84.7 5.7 %collective-permute-done.6.refs_1_ = f32[128,512]{1,0:T(8,128)S(1)} collective-permute-done((f32[128,512]{1,0:T(8,128)S(1)}, f32[128,512]{1,0:T(8,128)S(1)}, u32[]{:S(2)}, u32[]{:S(2)}) %collective-permute-start.6) | collective-permute-done | bytes 262176 | tf_op jit(solution)/shard_map/ppermute | solution.py:925
  90.4 6.8 %collective-permute-done.7.refs_2_ = f32[128,512]{1,0:T(8,128)S(1)} collective-permute-done((f32[128,512]{1,0:T(8,128)S(1)}, f32[128,512]{1,0:T(8,128)S(1)}, u32[]{:S(2)}, u32[]{:S(2)}) %collective-permute-start.7) | collective-permute-done | bytes 262176 | tf_op jit(solution)/shard_map/ppermute | solution.py:925
  102.1 4.2 %all-to-all-start.1 = ((f32[8,64,512]{2,1,0:T(8,128)}), f32[8,64,512]{2,1,0:T(8,128)}, u32[]{:S(2)}, u32[]{:S(2)}) async-start(f32[8,64,512]{2,1,0:T(8,128)} %copy-done.8), calls=%async_computation.1 | async-start | bytes 2097152 | tf_op jit(solution)/shard_map/all_to_all | solution.py:919
  112.9 3.8 %axial_stage.3.after.refs_6_ = f32[32,2,16,512]{3,2,1,0:T(8,128)} custom-call(s32[2]{0:T(128)S(1)} %copy-done.20, f32[32]{0:T(128)S(1)} %copy-done.22, f32[512,1]{1,0:T(8,128)S(1)} %copy.20.cyc, f32[1,512]{1,0:T(1,128)S(1)} %bitcast.4, f32[128,512]{1,0:T(8,128)S(1)} %copy-done.12, f32[128,512]{1,0:T(8,128)S(1)} %copy-done.14, f32[128,512]{1,0:T(8,128)S(1)} %copy-done.16, ...), custom_call_target="tpu_custom_call" | custom-call | flops 1 | bytes 1 | tf_op jit(solution)/shard_map/axial_stage/pallas_call | solution.py:802
  116.7 3.3 %cycle_stage.4 = (f32[128,512]{1,0:T(8,128)S(1)}, f32[128,512]{1,0:T(8,128)S(1)}, f32[128,512]{1,0:T(8,128)S(1)}, f32[128,512]{1,0:T(8,128)S(1)}) custom-call(s32[2]{0:T(128)S(1)} %copy-done.20, f32[8,64,512]{2,1,0:T(8,128)S(1)} %copy-done.5, bf16[1024,512]{1,0:T(8,128)(2,1)S(1)} %copy-done, f32[32,2,16,512]{3,2,1,0:T(8,128)} %axial_stage.3.after.refs_6_), custom_call_target="tpu_custom_call" | custom-call | flops 1 | bytes 1 | tf_op jit(solution)/shard_map/cycle_stage/pallas_call | solution.py:746
  124.0 5.6 %collective-permute-done.9.refs_1_ = f32[128,512]{1,0:T(8,128)S(1)} collective-permute-done((f32[128,512]{1,0:T(8,128)S(1)}, f32[128,512]{1,0:T(8,128)S(1)}, u32[]{:S(2)}, u32[]{:S(2)}) %collective-permute-start.9) | collective-permute-done | bytes 262176 | tf_op jit(solution)/shard_map/ppermute | solution.py:925
  129.6 6.8 %collective-permute-done.10.refs_2_ = f32[128,512]{1,0:T(8,128)S(1)} collective-permute-done((f32[128,512]{1,0:T(8,128)S(1)}, f32[128,512]{1,0:T(8,128)S(1)}, u32[]{:S(2)}, u32[]{:S(2)}) %collective-permute-start.10) | collective-permute-done | bytes 262176 | tf_op jit(solution)/shard_map/ppermute | solution.py:925
  136.4 3.8 %axial_stage.4.after = f32[32,2,16,512]{3,2,1,0:T(8,128)} custom-call(s32[2]{0:T(128)S(1)} %copy-done.20, f32[32]{0:T(128)S(1)} %copy-done.22, f32[512,1]{1,0:T(8,128)S(1)} %copy.20.cyc, f32[1,512]{1,0:T(1,128)S(1)} %bitcast.5, f32[128,512]{1,0:T(8,128)S(1)} %get-tuple-element.49.refs_0_.refs_5_, ...), custom_call_target="tpu_custom_call", output_to_operand_aliasing={{}: (10, {})} | custom-call | flops 1 | bytes 1 | tf_op jit(solution)/shard_map/axial_stage/pallas_call | solution.py:802
  140.2 4.8 %all-to-all-start.4 = ((f32[32,2,16,512]{3,2,1,0:T(8,128)}), f32[32,2,16,512]{3,2,1,0:T(8,128)}, u32[]{:S(2)}, u32[]{:S(2)}) async-start(f32[32,2,16,512]{3,2,1,0:T(8,128)} %axial_stage.4.after), calls=%async_computation.4 | async-start | bytes 4194304 | tf_op jit(solution)/shard_map/all_to_all | solution.py:919
  151.7 17.8 %collective-permute-done.12.refs_1_ = f32[128,512]{1,0:T(8,128)S(1)} collective-permute-done((f32[128,512]{1,0:T(8,128)S(1)}, f32[128,512]{1,0:T(8,128)S(1)}, u32[]{:S(2)}, u32[]{:S(2)}) %collective-permute-start.12) | collective-permute-done | bytes 262176 | tf_op jit(solution)/shard_map/ppermute | solution.py:925
  169.5 10.5 %collective-permute-done.14.refs_3_ = f32[128,512]{1,0:T(8,128)S(1)} collective-permute-done((f32[128,512]{1,0:T(8,128)S(1)}, f32[128,512]{1,0:T(8,128)S(1)}, u32[]{:S(2)}, u32[]{:S(2)}) %collective-permute-start.14) | collective-permute-done | bytes 262176 | tf_op jit(solution)/shard_map/ppermute | solution.py:925
  183.9 11.1 %all-to-all-done.4.piece = f32[32,2,16,512]{3,2,1,0:T(8,128)} async-done(((f32[32,2,16,512]{3,2,1,0:T(8,128)}), f32[32,2,16,512]{3,2,1,0:T(8,128)}, u32[]{:S(2)}, u32[]{:S(2)}) %all-to-all-start.4) | async-done | bytes 2097184 | tf_op jit(solution)/shard_map/all_to_all | solution.py:919
  194.9 3.4 %all-to-all-start.3 = ((f32[32,1,16,512]{3,2,1,0:T(8,128)}), f32[32,1,16,512]{3,2,1,0:T(8,128)}, u32[]{:S(2)}, u32[]{:S(2)}) async-start(f32[32,1,16,512]{3,2,1,0:T(8,128)} %copy-done.9), calls=%async_computation.3 | async-start | bytes 2097152 | tf_op jit(solution)/shard_map/all_to_all | solution.py:919
  199.4 4.8 %return_stage.3.refs_3_ = f32[3,16,16384]{2,1,0:T(8,128)} custom-call(f32[32,2,16,512]{3,2,1,0:T(8,128)} %all-to-all-done.4.piece, bf16[1024,512]{1,0:T(8,128)(2,1)S(1)} %copy-done, bf16[512,512]{1,0:T(8,128)(2,1)S(1)} %copy-done.2, bf16[1024,512]{1,0:T(8,128)(2,1)S(1)} %back_tables.1.refs_5_.refs_2_), custom_call_target="tpu_custom_call" | custom-call | flops 1 | bytes 1 | tf_op jit(solution)/shard_map/return_stage/pallas_call | solution.py:879
  204.2 4.9 %return_stage.4.refs_3_ = f32[3,16,16384]{2,1,0:T(8,128)} custom-call(f32[32,2,16,512]{3,2,1,0:T(8,128)} %all-to-all-done.4.piece, bf16[1024,512]{1,0:T(8,128)(2,1)S(1)} %copy-done, bf16[512,512]{1,0:T(8,128)(2,1)S(1)} %copy-done.2, bf16[1024,512]{1,0:T(8,128)(2,1)S(1)} %back_tables.1.refs_5_.refs_2_, ...), custom_call_target="tpu_custom_call", output_to_operand_aliasing={{}: (4, {})} | custom-call | flops 1 | bytes 1 | tf_op jit(solution)/shard_map/return_stage/pallas_call | solution.py:879
  209.1 16.7 %all-to-all-done.3.piece = f32[32,1,16,512]{3,2,1,0:T(8,128)} async-done(((f32[32,1,16,512]{3,2,1,0:T(8,128)}), f32[32,1,16,512]{3,2,1,0:T(8,128)}, u32[]{:S(2)}, u32[]{:S(2)}) %all-to-all-start.3) | async-done | bytes 1048608 | tf_op jit(solution)/shard_map/all_to_all | solution.py:919
  225.9 4.8 %return_stage.5 = f32[3,16,16384]{2,1,0:T(8,128)} custom-call(f32[32,1,16,512]{3,2,1,0:T(8,128)} %all-to-all-done.3.piece, bf16[1024,512]{1,0:T(8,128)(2,1)S(1)} %copy-done, bf16[512,512]{1,0:T(8,128)(2,1)S(1)} %copy-done.3, bf16[1024,512]{1,0:T(8,128)(2,1)S(1)} %back_tables.1.refs_5_.refs_2_, ...), custom_call_target="tpu_custom_call", output_to_operand_aliasing={{}: (4, {})} | custom-call | flops 1 | bytes 1 | tf_op jit(solution)/shard_map/return_stage/pallas_call | solution.py:879
  (94 shorter events, 54.2 us)
Async XLA Ops:
  3.2 23.0 %collective-permute-start.2 = (f32[128,512]{1,0:T(8,128)}, f32[128,512]{1,0:T(8,128)S(1)}, u32[]{:S(2)}, u32[]{:S(2)}) collective-permute-start(f32[128,512]{1,0:T(8,128)} %get-tuple-element.33), channel_id=1, source_target_pairs={{0,1},{1,2},{2,3},{3,4},{4,5},{5,6},{6,7},{7,0},{8,9},{9,10},{10,1... | collective-permute-start | bytes 786440 | tf_op jit(solution)/shard_map/ppermute | solution.py:980
  3.7 22.5 %collective-permute-start.4 = (f32[128,512]{1,0:T(8,128)}, f32[128,512]{1,0:T(8,128)S(1)}, u32[]{:S(2)}, u32[]{:S(2)}) collective-permute-start(f32[128,512]{1,0:T(8,128)} %get-tuple-element.36), channel_id=1, source_target_pairs={{1,0},{2,1},{3,2},{4,3},{5,4},{6,5},{7,6},{0,7},{9,8},{10,9},{11,1... | collective-permute-start | bytes 786440 | tf_op jit(solution)/shard_map/ppermute | solution.py:979
  7.8 8.1 %collective-permute-start = (f32[16,2048]{1,0:T(8,128)}, f32[16,2048]{1,0:T(8,128)S(1)}, u32[]{:S(2)}, u32[]{:S(2)}) collective-permute-start(f32[16,2048]{1,0:T(8,128)} %get-tuple-element.31), channel_id=1, source_target_pairs={{0,8},{8,16},{16,24},{1,9},{9,17},{17,25},{2,10},{10,18},{18,26},{... | collective-permute-start | bytes 393224 | tf_op jit(solution)/shard_map/ppermute | solution.py:978
  11.6 7.1 %collective-permute-start.1 = (f32[16,2048]{1,0:T(8,128)}, f32[16,2048]{1,0:T(8,128)S(1)}, u32[]{:S(2)}, u32[]{:S(2)}) collective-permute-start(f32[16,2048]{1,0:T(8,128)} %get-tuple-element.32), channel_id=1, source_target_pairs={{8,0},{16,8},{24,16},{9,1},{17,9},{25,17},{10,2},{18,10},{26,18},{... | collective-permute-start | bytes 393224 | tf_op jit(solution)/shard_map/ppermute | solution.py:977
  21.0 5.2 %collective-permute-start.3 = (f32[8,512]{1,0:T(8,128)}, f32[8,512]{1,0:T(8,128)S(1)}, u32[]{:S(2)}, u32[]{:S(2)}) collective-permute-start(f32[8,512]{1,0:T(8,128)} %get-tuple-element.35), channel_id=1, source_target_pairs={{0,1},{1,2},{2,3},{3,4},{4,5},{5,6},{6,7},{7,0},{8,9},{9,10},{10,1... | collective-permute-start | bytes 49160 | tf_op jit(solution)/shard_map/ppermute | solution.py:984
  21.0 5.2 %collective-permute-start.5 = (f32[8,512]{1,0:T(8,128)}, f32[8,512]{1,0:T(8,128)S(1)}, u32[]{:S(2)}, u32[]{:S(2)}) collective-permute-start(f32[8,512]{1,0:T(8,128)} %get-tuple-element.37), channel_id=1, source_target_pairs={{1,0},{2,1},{3,2},{4,3},{5,4},{6,5},{7,6},{0,7},{9,8},{10,9},{11,1... | collective-permute-start | bytes 49160 | tf_op jit(solution)/shard_map/ppermute | solution.py:983
  40.6 31.4 %all-to-all-start = ((f32[8,64,512]{2,1,0:T(8,128)}), f32[8,64,512]{2,1,0:T(8,128)S(1)}, u32[]{:S(2)}, u32[]{:S(2)}) async-start(f32[8,64,512]{2,1,0:T(8,128)} %stencil.2.rest_6_), calls=%async_computation | async-start | bytes 2097152 | tf_op jit(solution)/shard_map/all_to_all | solution.py:919
  45.4 30.2 %copy-start = (bf16[1024,512]{1,0:T(8,128)(2,1)S(1)}, bf16[1024,512]{1,0:T(8,128)(2,1)}, u32[]{:S(2)}) copy-start(bf16[1024,512]{1,0:T(8,128)(2,1)} %constant.14.clone.table_ref.refs_0_) | copy-start | bytes 3145732
  45.4 30.2 %copy-start.20 = (s32[2]{0:T(128)S(1)}, s32[2]{0:T(128)}, u32[]{:S(2)}) copy-start(s32[2]{0:T(128)} %pad_add_fusion.rest_6_.ids) | copy-start | bytes 28
  72.0 30.1 %all-to-all-start.2 = ((f32[8,64,512]{2,1,0:T(8,128)}), f32[8,64,512]{2,1,0:T(8,128)S(1)}, u32[]{:S(2)}, u32[]{:S(2)}) async-start(f32[8,64,512]{2,1,0:T(8,128)} %get-tuple-element.44.after), calls=%async_computation.2 | async-start | bytes 2097152 | tf_op jit(solution)/shard_map/all_to_all | solution.py:919
  80.8 25.5 %copy-start.29 = (f32[512]{0:T(512)S(1)}, f32[512]{0:T(512)}, u32[]{:S(2)}) copy-start(f32[512]{0:T(512)} %param.21) | copy-start | bytes 6148
  80.8 25.7 %copy-start.19 = (f32[32,32]{1,0:T(8,128)S(1)}, f32[32,32]{1,0:T(8,128)}, u32[]{:S(2)}) copy-start(f32[32,32]{1,0:T(8,128)} %basis_ref.3) | copy-start | bytes 12292
  80.8 9.5 %collective-permute-start.6 = (f32[128,512]{1,0:T(8,128)S(1)}, f32[128,512]{1,0:T(8,128)S(1)}, u32[]{:S(2)}, u32[]{:S(2)}) collective-permute-start(f32[128,512]{1,0:T(8,128)S(1)} %get-tuple-element.45), channel_id=1, source_target_pairs={{0,8},{8,0},{16,24},{24,16},{1,9},{9,1},{17,25},{25,17},{2,10},{10... | collective-permute-start | bytes 786440 | tf_op jit(solution)/shard_map/ppermute | solution.py:925
  83.3 13.9 %collective-permute-start.7 = (f32[128,512]{1,0:T(8,128)S(1)}, f32[128,512]{1,0:T(8,128)S(1)}, u32[]{:S(2)}, u32[]{:S(2)}) collective-permute-start(f32[128,512]{1,0:T(8,128)S(1)} %get-tuple-element.46), channel_id=1, source_target_pairs={{0,16},{8,24},{16,0},{24,8},{1,17},{9,25},{17,1},{25,9},{2,18},{10... | collective-permute-start | bytes 786440 | tf_op jit(solution)/shard_map/ppermute | solution.py:925
  83.3 13.9 %collective-permute-start.8 = (f32[128,512]{1,0:T(8,128)S(1)}, f32[128,512]{1,0:T(8,128)S(1)}, u32[]{:S(2)}, u32[]{:S(2)}) collective-permute-start(f32[128,512]{1,0:T(8,128)S(1)} %get-tuple-element.47), channel_id=1, source_target_pairs={{0,24},{8,16},{16,8},{24,0},{1,25},{9,17},{17,9},{25,1},{2,26},{10... | collective-permute-start | bytes 786440 | tf_op jit(solution)/shard_map/ppermute | solution.py:925
  102.1 38.2 %all-to-all-start.1 = ((f32[8,64,512]{2,1,0:T(8,128)}), f32[8,64,512]{2,1,0:T(8,128)}, u32[]{:S(2)}, u32[]{:S(2)}) async-start(f32[8,64,512]{2,1,0:T(8,128)} %copy-done.8), calls=%async_computation.1 | async-start | bytes 2097152 | tf_op jit(solution)/shard_map/all_to_all | solution.py:919
  120.0 9.6 %collective-permute-start.9 = (f32[128,512]{1,0:T(8,128)S(1)}, f32[128,512]{1,0:T(8,128)S(1)}, u32[]{:S(2)}, u32[]{:S(2)}) collective-permute-start(f32[128,512]{1,0:T(8,128)S(1)} %get-tuple-element.50), channel_id=1, source_target_pairs={{0,8},{8,0},{16,24},{24,16},{1,9},{9,1},{17,25},{25,17},{2,10},{10... | collective-permute-start | bytes 786440 | tf_op jit(solution)/shard_map/ppermute | solution.py:925
  122.5 13.9 %collective-permute-start.10 = (f32[128,512]{1,0:T(8,128)S(1)}, f32[128,512]{1,0:T(8,128)S(1)}, u32[]{:S(2)}, u32[]{:S(2)}) collective-permute-start(f32[128,512]{1,0:T(8,128)S(1)} %get-tuple-element.51), channel_id=1, source_target_pairs={{0,16},{8,24},{16,0},{24,8},{1,17},{9,25},{17,1},{25,9},{2,18},{10... | collective-permute-start | bytes 786440 | tf_op jit(solution)/shard_map/ppermute | solution.py:925
  122.5 13.9 %collective-permute-start.11 = (f32[128,512]{1,0:T(8,128)S(1)}, f32[128,512]{1,0:T(8,128)S(1)}, u32[]{:S(2)}, u32[]{:S(2)}) collective-permute-start(f32[128,512]{1,0:T(8,128)S(1)} %get-tuple-element.52), channel_id=1, source_target_pairs={{0,24},{8,16},{16,8},{24,0},{1,25},{9,17},{17,9},{25,1},{2,26},{10... | collective-permute-start | bytes 786440 | tf_op jit(solution)/shard_map/ppermute | solution.py:925
  140.2 54.7 %all-to-all-start.4 = ((f32[32,2,16,512]{3,2,1,0:T(8,128)}), f32[32,2,16,512]{3,2,1,0:T(8,128)}, u32[]{:S(2)}, u32[]{:S(2)}) async-start(f32[32,2,16,512]{3,2,1,0:T(8,128)} %axial_stage.4.after), calls=%async_computation.4 | async-start | bytes 4194304 | tf_op jit(solution)/shard_map/all_to_all | solution.py:919
  148.1 21.4 %collective-permute-start.12 = (f32[128,512]{1,0:T(8,128)S(1)}, f32[128,512]{1,0:T(8,128)S(1)}, u32[]{:S(2)}, u32[]{:S(2)}) collective-permute-start(f32[128,512]{1,0:T(8,128)S(1)} %get-tuple-element.54), channel_id=1, source_target_pairs={{0,8},{8,0},{16,24},{24,16},{1,9},{9,1},{17,25},{25,17},{2,10},{10... | collective-permute-start | bytes 786440 | tf_op jit(solution)/shard_map/ppermute | solution.py:925
  149.7 19.9 %collective-permute-start.13 = (f32[128,512]{1,0:T(8,128)S(1)}, f32[128,512]{1,0:T(8,128)S(1)}, u32[]{:S(2)}, u32[]{:S(2)}) collective-permute-start(f32[128,512]{1,0:T(8,128)S(1)} %get-tuple-element.55), channel_id=1, source_target_pairs={{0,16},{8,24},{16,0},{24,8},{1,17},{9,25},{17,1},{25,9},{2,18},{10... | collective-permute-start | bytes 786440 | tf_op jit(solution)/shard_map/ppermute | solution.py:925
  151.1 28.9 %collective-permute-start.14 = (f32[128,512]{1,0:T(8,128)S(1)}, f32[128,512]{1,0:T(8,128)S(1)}, u32[]{:S(2)}, u32[]{:S(2)}) collective-permute-start(f32[128,512]{1,0:T(8,128)S(1)} %get-tuple-element.56), channel_id=1, source_target_pairs={{0,24},{8,16},{16,8},{24,0},{1,25},{9,17},{17,9},{25,1},{2,26},{10... | collective-permute-start | bytes 786440 | tf_op jit(solution)/shard_map/ppermute | solution.py:925
  194.9 30.9 %all-to-all-start.3 = ((f32[32,1,16,512]{3,2,1,0:T(8,128)}), f32[32,1,16,512]{3,2,1,0:T(8,128)}, u32[]{:S(2)}, u32[]{:S(2)}) async-start(f32[32,1,16,512]{3,2,1,0:T(8,128)} %copy-done.9), calls=%async_computation.3 | async-start | bytes 2097152 | tf_op jit(solution)/shard_map/all_to_all | solution.py:919
  (26 other events, 109.4 us)
